TPU v7x, 32 devices: a whole 2x2x4 slice. The times are simulated.
32 devices in a mesh: ctx: 16 (over z, y, core), head: 2 (over x).
Axes of the slice: x: 2, y: 2, z: 4, core: 2. Of those that a mesh axis runs over, the one named last changes fastest.
Arguments:
- hidden_states: bfloat16 [8192, 5376], P('ctx', 'head'), may hold values from -6 to 6
- query_base: bfloat16 [8192, 4096], P('ctx', 'head'), may hold values from -8 to 8
- key_base: bfloat16 [8192, 2048], P('ctx', 'head'), may hold values from -8 to 8
- frozen_value_rows: bfloat16 [8192, 2048], P('ctx', 'head'), may hold values from -6 to 6
- query_down: bfloat16 [5376, 16], P('head'), may hold values from -0.078125 to 0.078125
- query_up: bfloat16 [16, 4096], P(None, 'head'), may hold values from -0.75 to 0.75
- value_down: bfloat16 [5376, 16], P('head'), may hold values from -0.078125 to 0.078125
- value_up_weight: bfloat16 [16, 2048], P(None, 'head'), may hold values from -0.75 to 0.75
- positions: int32 [8192], P('ctx'), may hold values from 0 to 16382, as said below
- block_mask: int32 [64, 9], replicated, may hold values from 0 to 1, as said below
- output_gradient: bfloat16 [8192, 4096], P('ctx', 'head'), may hold values from -96 to 96
Outputs:
- attention_out: bfloat16 [8192, 4096], P('ctx', 'head')
- grad_query_down: float32 [5376, 16], P('head')
- grad_query_up: float32 [16, 4096], P(None, 'head')
- grad_value_down: float32 [5376, 16], P('head')
- grad_value_up: float32 [16, 2048], P(None, 'head')
Inputs may be any that keep to these rules, and one draw needn't show every extreme that they name: positions rise strictly along the tokens. `block_mask`: entry (b, o) is 1 where the query block b may attend the key block b - o; column 0 is 1 in every row.
All inputs are finite; a program needn't handle non-finite values.
Results may differ from a plain program's by a relative error of at most 0.04.
Values may be sent and summed in bfloat16 or wider, within the bound.
No kernel may reach another device: no remote copies, remote signals or barrier semaphores. Data moves between devices by JAX's collectives and lax.ppermute only.
A program may use at most 192 MiB of HBM per device.

v0:
```python
import functools

import jax
import jax.numpy as jnp
import numpy as np
from jax import lax
from jax.experimental import pallas as pl
from jax.experimental.pallas import tpu as pltpu
from jax.sharding import PartitionSpec as P

D = 5376
QUERY_HEADS = 32
KEY_VALUE_HEADS = 16
HEAD_SIZE = 128
WINDOW = 1024
BLOCK = 128
GROUPS = QUERY_HEADS // KEY_VALUE_HEADS
GROUP_WIDTH = GROUPS * HEAD_SIZE
SCORE_SCALE = (D // QUERY_HEADS) ** (-0.5)
LOG2_E = 1.4426950408889634
ROPE_BASE = 10000.0
FORBIDDEN = -1e30
RANK = 16

SUB = 256
KEYS = SUB + WINDOW
LANES = 128
OFFSET_LANE = 64
ONES_LANE = RANK

CHUNKS = ((0, 2), (2, 6), (6, 8))
TOGETHER = (2, 2, 1)

ROWS_BY_COLS = (((1,), (0,)), ((), ()))
BOTH_MINOR = (((1,), (1,)), ((), ()))
BOTH_MAJOR = (((0,), (0,)), ((), ()))


def mm(left, right, dims=ROWS_BY_COLS):
    return lax.dot_general(left, right, dims, preferred_element_type=jnp.float32)


def swap_halves(x):
    return pltpu.roll(x, HEAD_SIZE // 2, 1)


def rotate_into(chunks, cosines, sines, key_ref, value_ref, outs):
    own = pl.ds(0, key_ref.shape[0])
    for (first, last), out_ref in zip(chunks, outs):
        count = last - first
        for head in range(first, last):
            cols = pl.ds(head * HEAD_SIZE, HEAD_SIZE)
            key = key_ref[:, cols].astype(jnp.float32)
            rotated = key * cosines + swap_halves(key) * sines
            out_ref[own, pl.ds((head - first) * HEAD_SIZE, HEAD_SIZE)] = rotated.astype(jnp.bfloat16)
            out_ref[own, pl.ds((count + head - first) * HEAD_SIZE, HEAD_SIZE)] = value_ref[:, cols]


def prologue_kernel(chunks, positions_ref, frequency_ref, key_ref, value_ref, cos_ref, sin_ref, *outs):
    half = HEAD_SIZE // 2
    angles = frequency_ref[...] * positions_ref[...].astype(jnp.float32)
    both = jnp.transpose(jnp.concatenate([jnp.cos(angles), jnp.sin(angles)], axis=0))
    turned = swap_halves(both)
    low_half = lax.broadcasted_iota(jnp.int32, both.shape, 1) < half
    cosines = jnp.where(low_half, both, turned)
    sines = jnp.where(low_half, -turned, both)
    cos_ref[...] = cosines
    sin_ref[...] = sines
    rotate_into(chunks, cosines, sines, key_ref, value_ref, outs)


def later_prologue_kernel(chunks, cos_ref, sin_ref, key_ref, value_ref, *outs):
    rotate_into(chunks, cos_ref[...], sin_ref[...], key_ref, value_ref, outs)


def attention_kernel(first, start, up_columns, place_ref, *refs):
    if first:
        mask_ref, *refs = refs
    (
        query_hbm,
        gradient_hbm,
        own_hbm,
        one_hbm,
        even_hbm,
        odd_hbm,
        query_up_ref,
        value_up_ref,
        query_low_ref,
        query_low_t_ref,
        cos_ref,
        sin_ref,
        *refs,
    ) = refs
    if not first:
        key_extra_hbm, value_extra_hbm, _, _, back_in, *refs = refs
    out_hbm, partial_hbm, back_ref, *refs = refs
    if first:
        key_extra_hbm, value_extra_hbm, *refs = refs
    (
        query_in,
        gradient_in,
        out_buf,
        up_query_buf,
        up_value_buf,
        low_buf,
        key_buf,
        value_buf,
        query_buf,
        gradient_buf,
        weight_buf,
        score_buf,
        product_buf,
        sems,
        head_sems,
    ) = refs
    heads = key_buf.shape[0]
    together = query_buf.shape[0]
    tokens = query_in.shape[1]
    keys = key_buf.shape[1]
    steps = tokens // SUB
    tiles = keys // SUB
    step_tiles = KEYS // SUB
    rows = GROUPS * SUB
    odd = place_ref[1] == 1

    def copy(source, target, sem):
        return pltpu.make_async_copy(source, target, sem)

    def start_far(even_source, odd_source, target, sem):
        @pl.when(odd)
        def _():
            copy(odd_source, target, sem).start()

        @pl.when(jnp.logical_not(odd))
        def _():
            copy(even_source, target, sem).start()

        return copy(even_source, target, sem)

    own_rows = pl.ds(0, tokens)
    low_copies = []
    if first:
        last = pl.ds(tokens, RANK)
        low_copies.append(start_far(even_hbm.at[last], odd_hbm.at[last], low_buf.at[0], sems.at[3]))
        for at, source in ((1, one_hbm), (2, own_hbm)):
            low_copies.append(copy(source.at[last], low_buf.at[at], sems.at[3 + at]))
            low_copies[-1].start()
    def wide_copy(hbm, buf, head, kind, out=False):
        cols = pl.ds(pl.multiple_of((start + head) * GROUP_WIDTH, GROUP_WIDTH), GROUP_WIDTH)
        ends = (buf.at[head], hbm.at[:, cols]) if out else (hbm.at[:, cols], buf.at[head])
        return copy(*ends, head_sems.at[head, 2, kind])

    for head in range(heads):
        wide_copy(query_hbm, query_in, head, 0).start()
        for kind, buf, at in ((0, key_buf, head), (1, value_buf, heads + head)):
            cols = pl.ds(at * HEAD_SIZE, HEAD_SIZE)
            main = pl.ds(0, HEAD_SIZE)
            sem = head_sems.at[head, kind]
            copies = [
                start_far(
                    even_hbm.at[own_rows, cols],
                    odd_hbm.at[own_rows, cols],
                    buf.at[head, pl.ds(0, tokens), main],
                    sem.at[0],
                ),
                copy(one_hbm.at[own_rows, cols], buf.at[head, pl.ds(tokens, tokens), main], sem.at[1]),
                copy(own_hbm.at[own_rows, cols], buf.at[head, pl.ds(2 * tokens, tokens), main], sem.at[2]),
            ]
            if not first:
                extra_hbm = (key_extra_hbm, value_extra_hbm)[kind]
                copies.append(copy(extra_hbm, buf.at[head, :, pl.ds(HEAD_SIZE, LANES)], sem.at[3]))
            for later in copies[1:]:
                later.start()
        wide_copy(gradient_hbm, gradient_in, head, 1).start()

    if first:
        first_block = place_ref[0] * (tokens // BLOCK)
        reach = WINDOW // BLOCK
        block_lane = lax.broadcasted_iota(jnp.int32, (BLOCK, LANES), 1)
        for key_block in range(keys // BLOCK):
            extra = jnp.where(block_lane == OFFSET_LANE, 1.0, 0.0)
            exists = first_block + (key_block - reach) >= 0
            for block in range(tokens // BLOCK):
                offset = reach + block - key_block
                if 0 <= offset <= reach:
                    hit = (mask_ref[offset, first_block + block] == 1) & exists
                    term = jnp.where(hit, 0.0, FORBIDDEN)
                else:
                    term = FORBIDDEN
                extra = jnp.where(block_lane == block, term, extra)
            for head in range(heads):
                key_buf[head, key_block * BLOCK : (key_block + 1) * BLOCK, HEAD_SIZE:] = extra.astype(
                    jnp.bfloat16
                )
        for low_copy in low_copies:
            low_copy.wait()
        low = jnp.concatenate([low_buf[at] for at in range(3)], axis=1)
        low = jnp.concatenate(
            [
                low.astype(jnp.float32),
                jnp.ones((2, keys), jnp.float32),
                jnp.zeros((LANES - RANK - 2, keys), jnp.float32),
            ],
            axis=0,
        )
        low = jnp.transpose(low).astype(jnp.bfloat16)
        for head in range(heads):
            value_buf[head, :, HEAD_SIZE:] = low
        extras = (
            copy(key_buf.at[0, :, pl.ds(HEAD_SIZE, LANES)], key_extra_hbm, sems.at[6]),
            copy(value_buf.at[0, :, pl.ds(HEAD_SIZE, LANES)], value_extra_hbm, sems.at[7]),
        )
        for extra_copy in extras:
            extra_copy.start()
        back_ref[...] = jnp.zeros_like(back_ref)
    else:
        extras = ()
        back_ref[...] = back_in[...]

    lane = lax.broadcasted_iota(jnp.int32, (rows, LANES), 1)
    row = lax.broadcasted_iota(jnp.int32, (rows, LANES), 0) % SUB
    ones = slice(HEAD_SIZE + ONES_LANE, HEAD_SIZE + ONES_LANE + 1)

    def own(step):
        return slice(step * SUB, (step + 1) * SUB)

    def span(step):
        return slice(step * rows, (step + 1) * rows)

    def window(step):
        return slice(step * SUB, step * SUB + KEYS)

    def tile_steps(tile):
        return max(0, tile - step_tiles + 1), min(steps, tile + 1)

    def member_cols(member):
        return slice(member * HEAD_SIZE, (member + 1) * HEAD_SIZE)

    def value_up_of(head):
        return jnp.concatenate(
            [value_up_ref[start + head], jnp.zeros((LANES - RANK, HEAD_SIZE), jnp.bfloat16)], axis=0
        )

    def limit(step, tile, part):
        place = tile - step
        if 0 < place < step_tiles - 1:
            return part
        halves = []
        for block in range(SUB // BLOCK):
            inside = lane > row % BLOCK if place == 0 else lane <= row % BLOCK
            inside = inside | (row // BLOCK != block)
            halves.append(
                jnp.where(inside, part[:, block * BLOCK : (block + 1) * BLOCK], FORBIDDEN)
            )
        return jnp.concatenate(halves, axis=1)

    def prepare(head, slot):
        reach_of_key = jnp.max(
            jnp.abs(key_buf[head, :, :HEAD_SIZE].astype(jnp.float32)), axis=0, keepdims=True
        )
        for step in range(steps):
            cosines = cos_ref[own(step), :]
            sines = sin_ref[own(step), :]
            adapted = mm(query_low_ref[own(step), :], query_up_ref[start + head])
            turned = []
            for member in range(GROUPS):
                part = query_in[head, own(step), member_cols(member)].astype(jnp.float32)
                part = part + adapted[:, member * HEAD_SIZE : (member + 1) * HEAD_SIZE]
                turned.append(part * cosines + swap_halves(part) * sines)
            queries = jnp.concatenate(turned, axis=0) * (SCORE_SCALE * LOG2_E)
            bound = jnp.sum(jnp.abs(queries) * reach_of_key, axis=1, keepdims=True)
            chosen = (lane == row // BLOCK + step * (SUB // BLOCK)).astype(jnp.float32)
            query_buf[slot, span(step), :HEAD_SIZE] = queries.astype(jnp.bfloat16)
            query_buf[slot, span(step), HEAD_SIZE:] = jnp.where(
                lane == OFFSET_LANE, -bound, chosen
            ).astype(jnp.bfloat16)

    def forward_scores(head, slot):
        for tile in range(tiles):
            low, high = tile_steps(tile)
            cols = slice(tile * SUB, (tile + 1) * SUB)
            scores = mm(
                query_buf[slot, low * rows : high * rows, :], key_buf[head, cols, :], BOTH_MINOR
            )
            for step in range(low, high):
                part = limit(step, tile, scores[(step - low) * rows : (step - low + 1) * rows, :])
                weight_buf[slot, span(step), cols] = jnp.exp2(part).astype(jnp.bfloat16)

    def forward_products(head, slot):
        for step in range(steps):
            product_buf[slot, span(step), :] = mm(
                weight_buf[slot, span(step), window(step)], value_buf[head, window(step), :]
            )

    def repeat(head, slot):
        diagonal = lane - row % BLOCK

        def one_step(step, carry):
            here = pl.ds(pl.multiple_of(step * rows, rows), rows)

            def scores_of(tile):
                cols = pl.ds(pl.multiple_of((step + tile) * SUB, SUB), SUB)
                part = mm(query_buf[slot, here, :], key_buf[head, cols, :], BOTH_MINOR)
                lowest = jnp.where(tile == 0, 1, -BLOCK)
                highest = jnp.where(tile == step_tiles - 1, 0, BLOCK)
                halves = []
                for block in range(SUB // BLOCK):
                    inside = (diagonal >= lowest) & (diagonal <= highest)
                    inside = inside | (row // BLOCK != block)
                    halves.append(
                        jnp.where(inside, part[:, block * BLOCK : (block + 1) * BLOCK], FORBIDDEN)
                    )
                return jnp.concatenate(halves, axis=1), cols

            def top(tile, highest):
                part, _ = scores_of(tile)
                return jnp.maximum(highest, jnp.max(part, axis=1, keepdims=True))

            def again(tile, sums):
                part, cols = scores_of(tile)
                weights = jnp.exp2(part).astype(jnp.bfloat16)
                weight_buf[slot, here, cols] = weights
                return sums + mm(weights, value_buf[head, cols, :])

            extra = query_buf[slot, here, HEAD_SIZE:].astype(jnp.float32)
            query_buf[slot, here, HEAD_SIZE:] = jnp.where(lane == OFFSET_LANE, 0.0, extra).astype(
                jnp.bfloat16
            )
            highest = lax.fori_loop(
                0, step_tiles, top, jnp.full((rows, 1), FORBIDDEN, jnp.float32)
            )
            query_buf[slot, here, HEAD_SIZE:] = jnp.where(lane == OFFSET_LANE, -highest, extra).astype(
                jnp.bfloat16
            )
            product_buf[slot, here, :] = lax.fori_loop(
                0, step_tiles, again, jnp.zeros((rows, HEAD_SIZE + LANES), jnp.float32)
            )
            return carry

        lax.fori_loop(0, steps, one_step, 0)

    kept = {}

    def finish_forward(head, slot):
        value_up = value_up_of(head)
        spreads = []
        inverses = []
        up_value = jnp.zeros((LANES, HEAD_SIZE), jnp.float32)
        for step in range(steps):
            gradient = jnp.concatenate(
                [gradient_in[head, own(step), member_cols(member)] for member in range(GROUPS)], axis=0
            )
            gradient_low = mm(gradient, value_up, BOTH_MINOR)
            inverse = 1.0 / product_buf[slot, span(step), ones]
            low_part = (product_buf[slot, span(step), HEAD_SIZE:] * inverse).astype(jnp.bfloat16)
            outputs = product_buf[slot, span(step), :HEAD_SIZE] * inverse + mm(low_part, value_up)
            outputs = outputs.astype(jnp.bfloat16)
            for member in range(GROUPS):
                out_buf[head, own(step), member_cols(member)] = outputs[own(member), :]
            delta = jnp.sum(
                outputs.astype(jnp.float32) * gradient.astype(jnp.float32), axis=1, keepdims=True
            )
            delta_high = delta.astype(jnp.bfloat16).astype(jnp.float32)
            extra = jnp.where(lane == ONES_LANE, -delta_high, gradient_low)
            extra = jnp.where(lane == ONES_LANE + 1, delta_high - delta, extra)
            gradient_buf[slot, span(step), :HEAD_SIZE] = gradient
            gradient_buf[slot, span(step), HEAD_SIZE:] = extra.astype(jnp.bfloat16)
            up_value += mm(low_part, gradient, BOTH_MAJOR)
            spreads.append(jnp.transpose(gradient_low * inverse)[:RANK, :].astype(jnp.bfloat16))
            inverses.append(inverse * SCORE_SCALE)
        up_value_buf[head] = up_value[:RANK, :].astype(jnp.bfloat16)
        wide_copy(out_hbm, out_buf, head, 2, out=True).start()
        kept[slot] = jnp.concatenate(spreads, axis=1), inverses

    def backward_scores(head, slot):
        spread = kept[slot][0]
        for tile in range(tiles):
            low, high = tile_steps(tile)
            cols = slice(tile * SUB, (tile + 1) * SUB)
            back_row = RANK + tile * SUB // tokens * RANK
            back_rows = slice(back_row, back_row + RANK)
            back_cols = slice(tile * SUB % tokens, tile * SUB % tokens + SUB)
            part = slice(low * rows, high * rows)
            grad_weights = mm(gradient_buf[slot, part, :], value_buf[head, cols, :], BOTH_MINOR)
            weights = weight_buf[slot, part, cols]
            score_buf[slot, part, cols] = weights * grad_weights.astype(jnp.bfloat16)
            back_ref[back_rows, back_cols] += mm(spread[:, part], weights)

    def backward_products(head, slot):
        query_grads = []
        for step in range(steps):
            cosines = cos_ref[own(step), :]
            sines = sin_ref[own(step), :]
            sums = mm(score_buf[slot, span(step), window(step)], key_buf[head, window(step), :HEAD_SIZE])
            sums = sums * kept[slot][1][step]
            turned = []
            for member in range(GROUPS):
                part = sums[own(member), :]
                turned.append(part * cosines - swap_halves(part) * sines)
            query_grads.append(jnp.concatenate(turned, axis=1).astype(jnp.bfloat16))
        query_grad = jnp.concatenate(query_grads, axis=0)
        up_query_buf[head] = mm(query_low_t_ref[...], query_grad).astype(jnp.bfloat16)
        back_ref[:RANK, :] += mm(query_up_ref[start + head], query_grad, BOTH_MINOR)

    def arrive(head, kind):
        buf = (key_buf, value_buf)[kind]
        main = pl.ds(0, HEAD_SIZE)
        source = one_hbm.at[own_rows, main]
        for part in range(3):
            copy(
                source, buf.at[head, pl.ds(part * tokens, tokens), main], head_sems.at[head, kind, part]
            ).wait()
        if not first:
            extra_hbm = (key_extra_hbm, value_extra_hbm)[kind]
            copy(
                extra_hbm, buf.at[head, :, pl.ds(HEAD_SIZE, LANES)], head_sems.at[head, kind, 3]
            ).wait()

    def arrive_and_prepare(head, slot):
        arrive(head, 0)
        wide_copy(query_hbm, query_in, head, 0).wait()
        prepare(head, slot)

    def work(group, carry):
        members = [(group * together + slot, slot) for slot in range(together)]
        arrive_and_prepare(*members[0])
        for head, slot in members:
            forward_scores(head, slot)
            if slot + 1 < together:
                arrive_and_prepare(*members[slot + 1])
            arrive(head, 1)
            forward_products(head, slot)

        @pl.when(jnp.min(product_buf[:, :, ones]) < 1e-18)
        def _():
            lax.fori_loop(0, together, lambda slot, c: (repeat(group * together + slot, slot), c)[1], 0)

        for head, slot in members:
            wide_copy(gradient_hbm, gradient_in, head, 1).wait()
        finish_forward(*members[0])
        for head, slot in members:
            backward_scores(head, slot)
            if slot + 1 < together:
                finish_forward(*members[slot + 1])
            backward_products(head, slot)
        return carry

    if heads == together:
        work(0, 0)
    else:
        lax.fori_loop(0, heads // together, work, 0)
    up_copies = []
    for head in range(heads):
        at = pl.ds((start + head) * GROUP_WIDTH, GROUP_WIDTH)
        up_copies.append(copy(up_query_buf.at[head], partial_hbm.at[:, at], head_sems.at[head, 3, 0]))
        at = pl.ds(up_columns + (start + head) * HEAD_SIZE, HEAD_SIZE)
        up_copies.append(copy(up_value_buf.at[head], partial_hbm.at[:, at], head_sems.at[head, 3, 1]))
    for up_copy in up_copies:
        up_copy.start()
    for head in range(heads):
        wide_copy(out_hbm, out_buf, head, 2, out=True).wait()
    for done in (*extras, *up_copies):
        done.wait()


VMEM = pl.BlockSpec(memory_space=pltpu.VMEM)
SMEM = pl.BlockSpec(memory_space=pltpu.SMEM)
ANY = pl.BlockSpec(memory_space=pl.ANY)
NEAR = 4


def attention_chunk(
    first, last, together, columns, place, mask, query_base, gradient, received, shared, tables, carried
):
    count = last - first
    tokens = query_base.shape[0]
    keys = 3 * tokens
    rows = GROUPS * tokens
    out_specs = [ANY, ANY, VMEM]
    out_shape = [
        jax.ShapeDtypeStruct(query_base.shape, jnp.bfloat16),
        jax.ShapeDtypeStruct((RANK, columns), jnp.bfloat16),
        jax.ShapeDtypeStruct((RANK + keys // tokens * RANK, tokens), jnp.float32),
    ]
    arguments = [place]
    in_specs = [SMEM]
    if carried is None:
        arguments.append(mask)
        in_specs.append(SMEM)
        out_specs += [ANY, ANY]
        out_shape += [jax.ShapeDtypeStruct((keys, LANES), jnp.bfloat16)] * 2
    arguments += [query_base, gradient, *received, *shared]
    in_specs += [ANY] * 6 + [VMEM] * len(shared)
    aliases = {}
    if carried is not None:
        arguments += [*tables, *carried]
        in_specs += [ANY, ANY, ANY, ANY, VMEM]
        aliases = {len(arguments) - 3: 0, len(arguments) - 2: 1}
    wide_buf = HEAD_SIZE + LANES
    return pl.pallas_call(
        functools.partial(attention_kernel, carried is None, first, query_base.shape[1]),
        in_specs=in_specs,
        out_specs=out_specs,
        scratch_shapes=[
            pltpu.VMEM((count, tokens, GROUP_WIDTH), jnp.bfloat16),
            pltpu.VMEM((count, tokens, GROUP_WIDTH), jnp.bfloat16),
            pltpu.VMEM((count, tokens, GROUP_WIDTH), jnp.bfloat16),
            pltpu.VMEM((count, RANK, GROUP_WIDTH), jnp.bfloat16),
            pltpu.VMEM((count, RANK, HEAD_SIZE), jnp.bfloat16),
            pltpu.VMEM((3, RANK, tokens), jnp.bfloat16),
            pltpu.VMEM((count, keys, wide_buf), jnp.bfloat16),
            pltpu.VMEM((count, keys, wide_buf), jnp.bfloat16),
            pltpu.VMEM((together, rows, wide_buf), jnp.bfloat16),
            pltpu.VMEM((together, rows, wide_buf), jnp.bfloat16),
            pltpu.VMEM((together, rows, keys), jnp.bfloat16),
            pltpu.VMEM((together, rows, keys), jnp.bfloat16),
            pltpu.VMEM((together, rows, wide_buf), jnp.float32),
            pltpu.SemaphoreType.DMA((10,)),
            pltpu.SemaphoreType.DMA((count, 4, 4)),
        ],
        out_shape=out_shape,
        input_output_aliases=aliases,
        compiler_params=pltpu.CompilerParams(vmem_limit_bytes=50 * 2**20),
    )(*arguments)


def down_kernel(first_column, back_ref, one_ref, two_ref, hidden_ref, _, partial_hbm, down_buf, sems):
    features = hidden_ref.shape[1]
    value_back = back_ref[3 * RANK :, :].astype(jnp.float32)
    value_back = value_back + one_ref[...].astype(jnp.float32) + two_ref[...].astype(jnp.float32)
    back = jnp.concatenate([back_ref[:RANK, :], value_back.astype(jnp.bfloat16)], axis=0)
    down_buf[...] = mm(back, hidden_ref[...]).astype(jnp.bfloat16)
    copies = [
        pltpu.make_async_copy(
            down_buf.at[pl.ds(at * RANK, RANK)],
            partial_hbm.at[:, pl.ds(first_column + at * features, features)],
            sems.at[at],
        )
        for at in range(2)
    ]
    for each in copies:
        each.start()
    for each in copies:
        each.wait()


def final_kernel(scale, place_ref, *refs):
    gathered = [ref[...].astype(jnp.float32) * scale for ref in refs[:NEAR]]
    query_up_ref, value_up_ref, query_down_ref, value_down_ref = refs[NEAR:]
    parts = []
    for at in range(NEAR):
        distance = (at % 2 * 2 + at // 2) ^ place_ref[0]
        part = gathered[0]
        for other in range(1, NEAR):
            part = jnp.where(distance == other, gathered[other], part)
        parts.append(part)
    total = jnp.concatenate(parts, axis=1)
    column = 0
    for ref in (query_up_ref, value_up_ref, query_down_ref, value_down_ref):
        ref[...] = total[:, column : column + ref.shape[1]]
        column += ref.shape[1]


def head_sum(x):
    if lax.axis_size("head") == 2:
        other = lax.ppermute(x, "head", [(0, 1), (1, 0)])
        return (x.astype(jnp.float32) + other.astype(jnp.float32)).astype(x.dtype)
    return lax.psum(x, "head")


def ctx_sum(x):
    devices = lax.axis_size("ctx")
    place = lax.axis_index("ctx") % NEAR

    def exchange(value, distance):
        return lax.ppermute(value, "ctx", [(i, i ^ distance) for i in range(devices)])

    def halve(value, bit, distance):
        half = value.shape[1] // 2
        kept = lax.dynamic_slice_in_dim(value, bit * half, half, 1)
        given = lax.dynamic_slice_in_dim(value, (1 - bit) * half, half, 1)
        return add(kept, exchange(given, distance))

    def add(one, other):
        return (one.astype(jnp.float32) + other.astype(jnp.float32)).astype(jnp.bfloat16)

    x = halve(x, place % 2, 1)
    x = halve(x, place // 2, 2)
    distance = NEAR
    while distance < devices:
        x = add(x, exchange(x, distance))
        distance *= 2
    return [x] + [exchange(x, distance) for distance in range(1, NEAR)]


def after(value, *others):
    return lax.optimization_barrier((value, *others))[0]


def per_device(
    hidden_states,
    query_base,
    key_base,
    frozen_value_rows,
    query_down,
    query_up,
    value_down,
    value_up_weight,
    positions,
    block_mask,
    output_gradient,
):
    tokens = hidden_states.shape[0]
    devices = lax.axis_size("ctx")
    device_index = lax.axis_index("ctx")
    kv_heads = key_base.shape[1] // HEAD_SIZE
    forward_one = [(i, i + 1) for i in range(devices - 1)]
    even_two = [(i, i + 2) for i in range(0, devices - 2, 2)]
    even_one = [(i, i + 1) for i in range(0, devices - 1, 2)]

    both_down = jnp.concatenate([query_down, value_down], axis=1)
    low = head_sum(mm(both_down, hidden_states, (((0,), (1,)), ((), ())))).astype(jnp.bfloat16)
    query_low_t = low[:RANK]
    value_low_t = low[RANK:]

    half = np.arange(HEAD_SIZE // 2, dtype=np.float64)
    frequency = (ROPE_BASE ** (-2.0 * half / HEAD_SIZE)).astype(np.float32)[:, None]

    def payload(chunk):
        first, last = chunk
        extra = RANK if first == 0 else 0
        return jax.ShapeDtypeStruct((tokens + extra, 2 * (last - first) * HEAD_SIZE), jnp.bfloat16)

    table = jax.ShapeDtypeStruct((tokens, HEAD_SIZE), jnp.float32)
    cosines, sines, packed_first = pl.pallas_call(
        functools.partial(prologue_kernel, CHUNKS[:1]),
        out_shape=[table, table, payload(CHUNKS[0])],
        compiler_params=pltpu.CompilerParams(vmem_limit_bytes=32 * 2**20),
    )(positions[None, :], jnp.asarray(frequency), key_base, frozen_value_rows)
    packed_first = lax.dynamic_update_slice(packed_first, value_low_t, (tokens, 0))
    packed_later = pl.pallas_call(
        functools.partial(later_prologue_kernel, CHUNKS[1:]),
        out_shape=[payload(chunk) for chunk in CHUNKS[1:]],
        compiler_params=pltpu.CompilerParams(vmem_limit_bytes=32 * 2**20),
    )(cosines, after(sines, packed_first), key_base, frozen_value_rows)
    packed = [packed_first, *packed_later]

    place = jnp.stack([device_index, device_index % 2]).astype(jnp.int32)
    query_ups = query_up.reshape(RANK, kv_heads, GROUP_WIDTH).transpose(1, 0, 2)
    value_ups = value_up_weight.reshape(RANK, kv_heads, HEAD_SIZE).transpose(1, 0, 2)
    shared = [query_ups, value_ups, query_low_t.T, query_low_t, cosines, sines]

    ones, evens = [], []
    for chunk, own in enumerate(packed):
        if chunk > 1:
            own = after(own, ones[chunk - 1], evens[chunk - 2])
        ones.append(lax.ppermute(own, "ctx", forward_one))
        evens.append(lax.ppermute(own, "ctx", even_two))

    features = hidden_states.shape[1]
    query_columns = kv_heads * GROUP_WIDTH
    value_columns = kv_heads * HEAD_SIZE
    columns = query_columns + value_columns + 2 * features
    columns = -(-columns // (NEAR * LANES)) * NEAR * LANES
    carried = None
    tables = None
    for chunk, (first, last) in enumerate(CHUNKS):
        one = ones[chunk]
        one = after(one, evens[0] if carried is None else carried[2])
        odd = lax.ppermute(one, "ctx", even_one)
        *carried, = attention_chunk(
            first,
            last,
            TOGETHER[chunk],
            columns,
            place,
            block_mask.T,
            query_base,
            output_gradient,
            [packed[chunk], one, evens[chunk], odd],
            shared,
            tables,
            carried,
        )
        if tables is None:
            tables = carried[3:]
            carried = carried[:3]
    attention_out, partial, back = carried

    back = head_sum(back.astype(jnp.bfloat16))
    back_one = lax.ppermute(
        back[2 * RANK : 3 * RANK], "ctx", [(i + 1, i) for i in range(devices - 1)]
    )
    back_two = lax.ppermute(back[RANK : 2 * RANK], "ctx", [(i + 2, i) for i in range(devices - 2)])
    arguments = [back, back_one, back_two, hidden_states, partial]
    partial = pl.pallas_call(
        functools.partial(down_kernel, query_columns + value_columns),
        in_specs=[VMEM] * (len(arguments) - 1) + [ANY],
        out_specs=ANY,
        out_shape=jax.ShapeDtypeStruct(partial.shape, partial.dtype),
        scratch_shapes=[
            pltpu.VMEM((2 * RANK, features), jnp.bfloat16),
            pltpu.SemaphoreType.DMA((2,)),
        ],
        input_output_aliases={len(arguments) - 1: 0},
        compiler_params=pltpu.CompilerParams(vmem_limit_bytes=32 * 2**20),
    )(*arguments)
    gathered = ctx_sum(partial)
    widths = (query_columns, value_columns, features, features)
    up_query, up_value, down_query, down_value = pl.pallas_call(
        functools.partial(final_kernel, float((devices * tokens) ** (-0.5))),
        in_specs=[SMEM] + [VMEM] * NEAR,
        out_specs=[VMEM] * 4,
        out_shape=[jax.ShapeDtypeStruct((RANK, width), jnp.float32) for width in widths],
    )((device_index % NEAR).astype(jnp.int32).reshape(1), *gathered)
    return attention_out, down_query.T, up_query, down_value.T, up_value


def solution(mesh):
    placed = (
        P("ctx", "head"),
        P("ctx", "head"),
        P("ctx", "head"),
        P("ctx", "head"),
        P("head", None),
        P(None, "head"),
        P("head", None),
        P(None, "head"),
        P("ctx"),
        P(),
        P("ctx", "head"),
    )
    return jax.shard_map(
        per_device,
        mesh=mesh,
        in_specs=placed,
        out_specs=(
            P("ctx", "head"),
            P("head", None),
            P(None, "head"),
            P("head", None),
            P(None, "head"),
        ),
        check_vma=False,
    )
```

profile of v0, /device:TPU:0, one launch (start us, length us, event | category | flops | bytes accessed | tf_op | source)
XLA Modules:
  0.0 205.9 jit_solution(6150367739908253701)
XLA Ops:
  0.7 2.9 %fusion = f32[32,512]{1,0:T(8,128)S(1)} fusion(bf16[512,2688]{1,0:T(8,128)(2,1)} %hidden_ref.1, bf16[2688,16]{0,1:T(8,128)(2,1)} %param.18, bf16[2688,16]{0,1:T(8,128)(2,1)} %param.16), kind=kOutput, calls=%fused_computation.1 | convolution fusion | flops 88424448 | bytes 2990080 | tf_op jit(solution)/shard_map/dot_general | solution.py:40
  3.6 3.0 %collective-permute-start = (f32[32,512]{1,0:T(8,128)S(1)}, f32[32,512]{1,0:T(8,128)S(1)}, u32[]{:S(2)}, u32[]{:S(2)}) collective-permute-start(f32[32,512]{1,0:T(8,128)S(1)} %fusion), channel_id=1, source_target_pairs={{0,1},{1,0},{2,3},{3,2},{4,5},{5,4},{6,7},{7,6},{8,9},{9,8},{10,11... | collective-permute-start | bytes 196616 | tf_op jit(solution)/shard_map/ppermute | solution.py:566
  7.4 1.4 collective-permute-done
  9.4 4.0 %collective-permute-start.2 = (bf16[528,512]{1,0:T(8,128)(2,1)S(1)}, bf16[528,512]{1,0:T(8,128)(2,1)S(1)}, u32[]{:S(2)}, u32[]{:S(2)}) collective-permute-start(bf16[528,512]{1,0:T(8,128)(2,1)S(1)} %get-tuple-element.59.refs_3_), channel_id=1, source_target_pairs={{0,4},{4,8},{8,12},{12,16},{16,20},{20,24},{24,28},{1,5},{5,9},{9,... | collective-permute-start | bytes 1622024 | tf_op jit(solution)/shard_map/ppermute | solution.py:658
  13.4 1.3 collective-permute-start.4
  16.1 5.1 %collective-permute-start.1 = (bf16[512,1024]{1,0:T(8,128)(2,1)S(1)}, bf16[512,1024]{1,0:T(8,128)(2,1)}, u32[]{:S(2)}, u32[]{:S(2)}) collective-permute-start(bf16[512,1024]{1,0:T(8,128)(2,1)S(1)} %get-tuple-element.35.refs_2_), channel_id=1, source_target_pairs={{0,2},{2,4},{4,6},{6,8},{8,10},{10,12},{12,14},{14,16},{16,18},{18... | collective-permute-start | bytes 3145736 | tf_op jit(solution)/shard_map/ppermute | solution.py:657
  21.1 2.0 collective-permute-done.2.refs_5_
  23.1 5.7 %collective-permute-start.5 = (bf16[528,512]{1,0:T(8,128)(2,1)S(1)}, bf16[528,512]{1,0:T(8,128)(2,1)}, u32[]{:S(2)}, u32[]{:S(2)}) collective-permute-start(bf16[528,512]{1,0:T(8,128)(2,1)S(1)} %collective-permute-done.4.refs_4_), channel_id=1, source_target_pairs={{0,2},{4,6},{8,10},{12,14},{16,18},{20,22},{24,26},{28,30},{1,3},{... | collective-permute-start | bytes 1622024 | tf_op jit(solution)/shard_map/ppermute | solution.py:670
  29.4 4.7 %collective-permute-start.6 = (bf16[512,1024]{1,0:T(8,128)(2,1)S(1)}, bf16[512,1024]{1,0:T(8,128)(2,1)}, u32[]{:S(2)}, u32[]{:S(2)}) collective-permute-start(bf16[512,1024]{1,0:T(8,128)(2,1)S(1)} %get-tuple-element.35.refs_2_), channel_id=1, source_target_pairs={{0,4},{4,8},{8,12},{12,16},{16,20},{20,24},{24,28},{1,5},{5,9},{9,... | collective-permute-start | bytes 3145736 | tf_op jit(solution)/shard_map/ppermute | solution.py:658
  37.4 29.5 %shard_map.157 = (bf16[512,2048]{1,0:T(8,128)(2,1)}, bf16[16,8704]{1,0:T(8,128)(2,1)S(1)}, f32[64,512]{1,0:T(8,128)S(1)}, bf16[1536,128]{1,0:T(8,128)(2,1)S(1)}, bf16[1536,128]{1,0:T(8,128)(2,1)S(1)}) custom-call(s32[2]{0:T(128)S(1)} %copy-done.14, s32[9,64]{1,0:T(8,128)S(1)} %bitcast.27, bf16[512,2048]{1,0:T(8,128)(2,1)} %refs_0_.3, ...), custom_call_target="tpu_custom_call" | custom-call | tf_op jit(solution)/shard_map/pallas_call | solution.py:500
  66.9 1.4 collective-permute-start.7
  68.2 1.3 collective-permute-start.3
  69.6 4.2 %collective-permute-start.8 = (bf16[512,512]{1,0:T(8,128)(2,1)S(1)}, bf16[512,512]{1,0:T(8,128)(2,1)S(1)}, u32[]{:S(2)}, u32[]{:S(2)}) collective-permute-start(bf16[512,512]{1,0:T(8,128)(2,1)S(1)} %copy-done.9), channel_id=1, source_target_pairs={{0,4},{4,8},{8,12},{12,16},{16,20},{20,24},{24,28},{1,5},{5,9},{9,... | collective-permute-start | bytes 1572872 | tf_op jit(solution)/shard_map/ppermute | solution.py:658
  74.8 57.5 %shard_map.158 = (bf16[512,2048]{1,0:T(8,128)(2,1)}, bf16[16,8704]{1,0:T(8,128)(2,1)S(1)}, f32[64,512]{1,0:T(8,128)S(1)}) custom-call(s32[2]{0:T(128)S(1)} %copy-done.14, bf16[512,2048]{1,0:T(8,128)(2,1)} %refs_0_.3, bf16[512,2048]{1,0:T(8,128)(2,1)} %refs_1_.5, ...), custom_call_target="tpu_custom_call", output_to_operand_aliasing={{0}: (15, {}), {1}: (16, {})} | custom-call | tf_op jit(solution)/shard_map/pallas_call | solution.py:500
  132.2 1.3 collective-permute-start.9
  133.6 1.5 collective-permute-done.9.refs_5_
  136.8 31.8 %shard_map.159 = (bf16[512,2048]{1,0:T(8,128)(2,1)}, bf16[16,8704]{1,0:T(8,128)(2,1)S(1)}, f32[64,512]{1,0:T(8,128)S(1)}) custom-call(s32[2]{0:T(128)S(1)} %copy-done.15, bf16[512,2048]{1,0:T(8,128)(2,1)} %refs_0_.3, bf16[512,2048]{1,0:T(8,128)(2,1)} %refs_1_.5, bf16[512,512]{1,0:T(8,128)(2,1)S(1)} %copy-done.9, ...), custom_call_target="tpu_custom_call", output_to_operand_aliasing={{0}: (15, {}), {1}: (16, {})} | custom-call | tf_op jit(solution)/shard_map/pallas_call | solution.py:500
  168.6 1.5 collective-permute-start.10
  170.2 2.9 %collective-permute-done.10 = bf16[64,512]{1,0:T(8,128)(2,1)S(1)} collective-permute-done((bf16[64,512]{1,0:T(8,128)(2,1)S(1)}, bf16[64,512]{1,0:T(8,128)(2,1)S(1)}, u32[]{:S(2)}, u32[]{:S(2)}) %collective-permute-start.10) | collective-permute-done | bytes 65568 | tf_op jit(solution)/shard_map/ppermute | solution.py:566
  173.2 1.3 collective-permute-start.11
  174.5 1.3 collective-permute-start.12
  176.3 3.9 %collective-permute-done.12.two_ref = bf16[16,512]{1,0:T(8,128)(2,1)S(1)} collective-permute-done((bf16[16,512]{1,0:T(8,128)(2,1)S(1)}, bf16[16,512]{1,0:T(8,128)(2,1)S(1)}, u32[]{:S(2)}, u32[]{:S(2)}) %collective-permute-start.12) | collective-permute-done | bytes 16416 | tf_op jit(solution)/shard_map/ppermute | solution.py:694
  182.3 2.8 %collective-permute-start.14 = (bf16[16,2176]{1,0:T(8,128)(2,1)S(1)}, bf16[16,2176]{1,0:T(8,128)(2,1)S(1)}, u32[]{:S(2)}, u32[]{:S(2)}) collective-permute-start(bf16[16,2176]{1,0:T(8,128)(2,1)S(1)} %constant_dynamic-slice_fusion), channel_id=1, source_target_pairs={{0,4},{2,6},{4,0},{6,2},{8,12},{10,14},{12,8},{14,10},{16,20},{18,... | collective-permute-start | bytes 208904 | tf_op jit(solution)/shard_map/ppermute | solution.py:576
  185.2 2.5 %collective-permute-done.14 = bf16[16,2176]{1,0:T(8,128)(2,1)S(1)} collective-permute-done((bf16[16,2176]{1,0:T(8,128)(2,1)S(1)}, bf16[16,2176]{1,0:T(8,128)(2,1)S(1)}, u32[]{:S(2)}, u32[]{:S(2)}) %collective-permute-start.14) | collective-permute-done | bytes 69664 | tf_op jit(solution)/shard_map/ppermute | solution.py:576
  187.7 1.6 collective-permute-start.15
  189.3 2.8 %collective-permute-done.15 = bf16[16,2176]{1,0:T(8,128)(2,1)S(1)} collective-permute-done((bf16[16,2176]{1,0:T(8,128)(2,1)S(1)}, bf16[16,2176]{1,0:T(8,128)(2,1)S(1)}, u32[]{:S(2)}, u32[]{:S(2)}) %collective-permute-start.15) | collective-permute-done | bytes 69664 | tf_op jit(solution)/shard_map/ppermute | solution.py:576
  192.1 2.6 %collective-permute-start.16 = (bf16[16,2176]{1,0:T(8,128)(2,1)S(1)}, bf16[16,2176]{1,0:T(8,128)(2,1)S(1)}, u32[]{:S(2)}, u32[]{:S(2)}) collective-permute-start(bf16[16,2176]{1,0:T(8,128)(2,1)S(1)} %add_convert_fusion.2), channel_id=1, source_target_pairs={{0,16},{2,18},{4,20},{6,22},{8,24},{10,26},{12,28},{14,30},{16,0},... | collective-permute-start | bytes 208904 | tf_op jit(solution)/shard_map/ppermute | solution.py:576
  194.7 2.6 %collective-permute-done.16 = bf16[16,2176]{1,0:T(8,128)(2,1)S(1)} collective-permute-done((bf16[16,2176]{1,0:T(8,128)(2,1)S(1)}, bf16[16,2176]{1,0:T(8,128)(2,1)S(1)}, u32[]{:S(2)}, u32[]{:S(2)}) %collective-permute-start.16) | collective-permute-done | bytes 69664 | tf_op jit(solution)/shard_map/ppermute | solution.py:576
  197.5 1.9 collective-permute-start.18
  199.4 2.7 %collective-permute-done.18.refs_2_ = bf16[16,2176]{1,0:T(8,128)(2,1)S(1)} collective-permute-done((bf16[16,2176]{1,0:T(8,128)(2,1)S(1)}, bf16[16,2176]{1,0:T(8,128)(2,1)S(1)}, u32[]{:S(2)}, u32[]{:S(2)}) %collective-permute-start.18) | collective-permute-done | bytes 69664 | tf_op jit(solution)/shard_map/ppermute | solution.py:576
  202.1 1.4 collective-permute-done.19.refs_3_
  204.1 1.8 shard_map.161
  (79 shorter events, 12.8 us)
Async XLA Ops:
  0.6 28.8 %copy-start = (bf16[16,1024]{1,0:T(8,128)(2,1)S(1)}, bf16[16,1024]{1,0:T(8,128)(2,1)}, u32[]{:S(2)}) copy-start(bf16[16,1024]{1,0:T(8,128)(2,1)} %param.19) | copy-start | bytes 98308
  0.6 5.9 %copy-start.12 = (f32[64,1]{1,0:T(8,128)S(1)}, f32[64,1]{1,0:T(8,128)}, u32[]{:S(2)}) copy-start(f32[64,1]{1,0:T(8,128)} %constant.58.clone.frequency_ref) | copy-start | bytes 772
  0.7 5.9 %copy-start.16 = (s32[512]{0:T(512)S(1)}, s32[512]{0:T(512)}, u32[]{:S(2)}) copy-start(s32[512]{0:T(512)} %param.20) | copy-start | bytes 6148
  0.7 5.9 %copy-start.2 = (bf16[512,1024]{1,0:T(8,128)(2,1)S(1)}, bf16[512,1024]{1,0:T(8,128)(2,1)}, u32[]{:S(2)}) copy-start(bf16[512,1024]{1,0:T(8,128)(2,1)} %key_ref.3) | copy-start | bytes 3145732
  3.6 5.2 %collective-permute-start = (f32[32,512]{1,0:T(8,128)S(1)}, f32[32,512]{1,0:T(8,128)S(1)}, u32[]{:S(2)}, u32[]{:S(2)}) collective-permute-start(f32[32,512]{1,0:T(8,128)S(1)} %fusion), channel_id=1, source_target_pairs={{0,1},{1,0},{2,3},{3,2},{4,5},{5,4},{6,7},{7,6},{8,9},{9,8},{10,11... | collective-permute-start | bytes 196616 | tf_op jit(solution)/shard_map/ppermute | solution.py:566
  6.6 22.3 %copy-start.23 = (bf16[16,2048]{1,0:T(8,128)(2,1)S(1)}, bf16[16,2048]{1,0:T(8,128)(2,1)}, u32[]{:S(2)}) copy-start(bf16[16,2048]{1,0:T(8,128)(2,1)} %param.17) | copy-start | bytes 196612
  7.4 66.4 %copy-start.4 = (f32[512,128]{1,0:T(8,128)}, f32[512,128]{1,0:T(8,128)S(1)}, u32[]{:S(2)}) copy-start(f32[512,128]{1,0:T(8,128)S(1)} %get-tuple-element.33.sin_ref.refs_12_.refs_11_) | copy-start | bytes 786436
  9.4 24.8 %copy-start.6 = (bf16[528,512]{1,0:T(8,128)(2,1)}, bf16[528,512]{1,0:T(8,128)(2,1)S(1)}, u32[]{:S(2)}) copy-start(bf16[528,512]{1,0:T(8,128)(2,1)S(1)} %get-tuple-element.59.refs_3_) | copy-start | bytes 1622020
  9.4 13.7 %collective-permute-start.2 = (bf16[528,512]{1,0:T(8,128)(2,1)S(1)}, bf16[528,512]{1,0:T(8,128)(2,1)S(1)}, u32[]{:S(2)}, u32[]{:S(2)}) collective-permute-start(bf16[528,512]{1,0:T(8,128)(2,1)S(1)} %get-tuple-element.59.refs_3_), channel_id=1, source_target_pairs={{0,4},{4,8},{8,12},{12,16},{16,20},{20,24},{24,28},{1,5},{5,9},{9,... | collective-permute-start | bytes 1622024 | tf_op jit(solution)/shard_map/ppermute | solution.py:658
  13.4 9.7 %collective-permute-start.4 = (bf16[528,512]{1,0:T(8,128)(2,1)S(1)}, bf16[528,512]{1,0:T(8,128)(2,1)S(1)}, u32[]{:S(2)}, u32[]{:S(2)}) collective-permute-start(bf16[528,512]{1,0:T(8,128)(2,1)S(1)} %get-tuple-element.59.refs_3_), channel_id=1, source_target_pairs={{0,2},{2,4},{4,6},{6,8},{8,10},{10,12},{12,14},{14,16},{16,18},{18... | collective-permute-start | bytes 1622024 | tf_op jit(solution)/shard_map/ppermute | solution.py:657
  16.1 50.8 %collective-permute-start.1 = (bf16[512,1024]{1,0:T(8,128)(2,1)S(1)}, bf16[512,1024]{1,0:T(8,128)(2,1)}, u32[]{:S(2)}, u32[]{:S(2)}) collective-permute-start(bf16[512,1024]{1,0:T(8,128)(2,1)S(1)} %get-tuple-element.35.refs_2_), channel_id=1, source_target_pairs={{0,2},{2,4},{4,6},{6,8},{8,10},{10,12},{12,14},{14,16},{16,18},{18... | collective-permute-start | bytes 3145736 | tf_op jit(solution)/shard_map/ppermute | solution.py:657
  23.1 11.1 %collective-permute-start.5 = (bf16[528,512]{1,0:T(8,128)(2,1)S(1)}, bf16[528,512]{1,0:T(8,128)(2,1)}, u32[]{:S(2)}, u32[]{:S(2)}) collective-permute-start(bf16[528,512]{1,0:T(8,128)(2,1)S(1)} %collective-permute-done.4.refs_4_), channel_id=1, source_target_pairs={{0,2},{4,6},{8,10},{12,14},{16,18},{20,22},{24,26},{28,30},{1,3},{... | collective-permute-start | bytes 1622024 | tf_op jit(solution)/shard_map/ppermute | solution.py:670
  29.4 44.3 %collective-permute-start.6 = (bf16[512,1024]{1,0:T(8,128)(2,1)S(1)}, bf16[512,1024]{1,0:T(8,128)(2,1)}, u32[]{:S(2)}, u32[]{:S(2)}) collective-permute-start(bf16[512,1024]{1,0:T(8,128)(2,1)S(1)} %get-tuple-element.35.refs_2_), channel_id=1, source_target_pairs={{0,4},{4,8},{8,12},{12,16},{16,20},{20,24},{24,28},{1,5},{5,9},{9,... | collective-permute-start | bytes 3145736 | tf_op jit(solution)/shard_map/ppermute | solution.py:658
  37.4 30.9 %copy-start.9 = (bf16[512,512]{1,0:T(8,128)(2,1)S(1)}, bf16[512,512]{1,0:T(8,128)(2,1)}, u32[]{:S(2)}) copy-start(bf16[512,512]{1,0:T(8,128)(2,1)} %copy-done.8) | copy-start | bytes 1572868
  37.4 37.4 %copy-start.11 = (bf16[16,512]{1,0:T(8,128)(2,1)S(1)}, bf16[16,512]{1,0:T(8,128)(2,1)}, u32[]{:S(2)}) copy-start(bf16[16,512]{1,0:T(8,128)(2,1)} %get-tuple-element.57.refs_10_.refs_9_) | copy-start | bytes 49156
  66.9 6.9 %collective-permute-start.7 = (bf16[512,1024]{1,0:T(8,128)(2,1)}, bf16[512,1024]{1,0:T(8,128)(2,1)S(1)}, u32[]{:S(2)}, u32[]{:S(2)}) collective-permute-start(bf16[512,1024]{1,0:T(8,128)(2,1)} %collective-permute-done.1.refs_3_), channel_id=1, source_target_pairs={{0,2},{4,6},{8,10},{12,14},{16,18},{20,22},{24,26},{28,30},{1,3},{... | collective-permute-start | bytes 3145736 | tf_op jit(solution)/shard_map/ppermute | solution.py:670
  68.2 64.0 %collective-permute-start.3 = (bf16[512,512]{1,0:T(8,128)(2,1)S(1)}, bf16[512,512]{1,0:T(8,128)(2,1)S(1)}, u32[]{:S(2)}, u32[]{:S(2)}) collective-permute-start(bf16[512,512]{1,0:T(8,128)(2,1)S(1)} %copy-done.9), channel_id=1, source_target_pairs={{0,2},{2,4},{4,6},{6,8},{8,10},{10,12},{12,14},{14,16},{16,18},{18... | collective-permute-start | bytes 1572872 | tf_op jit(solution)/shard_map/ppermute | solution.py:657
  69.6 64.0 %collective-permute-start.8 = (bf16[512,512]{1,0:T(8,128)(2,1)S(1)}, bf16[512,512]{1,0:T(8,128)(2,1)S(1)}, u32[]{:S(2)}, u32[]{:S(2)}) collective-permute-start(bf16[512,512]{1,0:T(8,128)(2,1)S(1)} %copy-done.9), channel_id=1, source_target_pairs={{0,4},{4,8},{8,12},{12,16},{16,20},{20,24},{24,28},{1,5},{5,9},{9,... | collective-permute-start | bytes 1572872 | tf_op jit(solution)/shard_map/ppermute | solution.py:658
  74.8 61.1 %copy-start.15 = (s32[2]{0:T(128)S(1)}, s32[2]{0:T(128)}, u32[]{:S(2)}) copy-start(s32[2]{0:T(128)} %pad_add_fusion.place_ref) | copy-start | bytes 28
  132.2 2.8 %collective-permute-start.9 = (bf16[512,512]{1,0:T(8,128)(2,1)S(1)}, bf16[512,512]{1,0:T(8,128)(2,1)S(1)}, u32[]{:S(2)}, u32[]{:S(2)}) collective-permute-start(bf16[512,512]{1,0:T(8,128)(2,1)S(1)} %collective-permute-done.3.refs_3_), channel_id=1, source_target_pairs={{0,2},{4,6},{8,10},{12,14},{16,18},{20,22},{24,26},{28,30},{1,3},{... | collective-permute-start | bytes 1572872 | tf_op jit(solution)/shard_map/ppermute | solution.py:670
  136.8 43.3 %copy-start.1 = (bf16[512,2688]{1,0:T(8,128)(2,1)S(1)}, bf16[512,2688]{1,0:T(8,128)(2,1)}, u32[]{:S(2)}) copy-start(bf16[512,2688]{1,0:T(8,128)(2,1)} %hidden_ref.1) | copy-start | bytes 8257540
  168.6 4.5 %collective-permute-start.10 = (bf16[64,512]{1,0:T(8,128)(2,1)S(1)}, bf16[64,512]{1,0:T(8,128)(2,1)S(1)}, u32[]{:S(2)}, u32[]{:S(2)}) collective-permute-start(bf16[64,512]{1,0:T(8,128)(2,1)S(1)} %convert_element_type.52), channel_id=1, source_target_pairs={{0,1},{1,0},{2,3},{3,2},{4,5},{5,4},{6,7},{7,6},{8,9},{9,8},{10,11... | collective-permute-start | bytes 196616 | tf_op jit(solution)/shard_map/ppermute | solution.py:566
  173.2 3.1 %collective-permute-start.11 = (bf16[16,512]{1,0:T(8,128)(2,1)S(1)}, bf16[16,512]{1,0:T(8,128)(2,1)S(1)}, u32[]{:S(2)}, u32[]{:S(2)}) collective-permute-start(bf16[16,512]{1,0:T(8,128)(2,1)S(1)} %get-tuple-element.56), channel_id=1, source_target_pairs={{2,0},{4,2},{6,4},{8,6},{10,8},{12,10},{14,12},{16,14},{18,16},{20... | collective-permute-start | bytes 49160 | tf_op jit(solution)/shard_map/ppermute | solution.py:691
  174.5 5.6 %collective-permute-start.12 = (bf16[16,512]{1,0:T(8,128)(2,1)S(1)}, bf16[16,512]{1,0:T(8,128)(2,1)S(1)}, u32[]{:S(2)}, u32[]{:S(2)}) collective-permute-start(bf16[16,512]{1,0:T(8,128)(2,1)S(1)} %get-tuple-element.55), channel_id=1, source_target_pairs={{4,0},{6,2},{8,4},{10,6},{12,8},{14,10},{16,12},{18,14},{20,16},{2... | collective-permute-start | bytes 49160 | tf_op jit(solution)/shard_map/ppermute | solution.py:694
  180.9 1.4 collective-permute-start.13
  182.3 5.3 %collective-permute-start.14 = (bf16[16,2176]{1,0:T(8,128)(2,1)S(1)}, bf16[16,2176]{1,0:T(8,128)(2,1)S(1)}, u32[]{:S(2)}, u32[]{:S(2)}) collective-permute-start(bf16[16,2176]{1,0:T(8,128)(2,1)S(1)} %constant_dynamic-slice_fusion), channel_id=1, source_target_pairs={{0,4},{2,6},{4,0},{6,2},{8,12},{10,14},{12,8},{14,10},{16,20},{18,... | collective-permute-start | bytes 208904 | tf_op jit(solution)/shard_map/ppermute | solution.py:576
  187.7 4.4 %collective-permute-start.15 = (bf16[16,2176]{1,0:T(8,128)(2,1)S(1)}, bf16[16,2176]{1,0:T(8,128)(2,1)S(1)}, u32[]{:S(2)}, u32[]{:S(2)}) collective-permute-start(bf16[16,2176]{1,0:T(8,128)(2,1)S(1)} %add_convert_fusion.3), channel_id=1, source_target_pairs={{0,8},{2,10},{4,12},{6,14},{8,0},{10,2},{12,4},{14,6},{16,24},{18,... | collective-permute-start | bytes 208904 | tf_op jit(solution)/shard_map/ppermute | solution.py:576
  192.1 5.3 %collective-permute-start.16 = (bf16[16,2176]{1,0:T(8,128)(2,1)S(1)}, bf16[16,2176]{1,0:T(8,128)(2,1)S(1)}, u32[]{:S(2)}, u32[]{:S(2)}) collective-permute-start(bf16[16,2176]{1,0:T(8,128)(2,1)S(1)} %add_convert_fusion.2), channel_id=1, source_target_pairs={{0,16},{2,18},{4,20},{6,22},{8,24},{10,26},{12,28},{14,30},{16,0},... | collective-permute-start | bytes 208904 | tf_op jit(solution)/shard_map/ppermute | solution.py:576
  197.4 6.1 %copy-start.19 = (bf16[16,2176]{1,0:T(8,128)(2,1)}, bf16[16,2176]{1,0:T(8,128)(2,1)S(1)}, u32[]{:S(2)}) copy-start(bf16[16,2176]{1,0:T(8,128)(2,1)S(1)} %add_convert_fusion.1.refs_0_) | copy-start | bytes 208900
  197.4 2.0 collective-permute-start.17
  197.5 4.7 %collective-permute-start.18 = (bf16[16,2176]{1,0:T(8,128)(2,1)S(1)}, bf16[16,2176]{1,0:T(8,128)(2,1)S(1)}, u32[]{:S(2)}, u32[]{:S(2)}) collective-permute-start(bf16[16,2176]{1,0:T(8,128)(2,1)S(1)} %add_convert_fusion.1.refs_0_), channel_id=1, source_target_pairs={{0,4},{2,6},{4,0},{6,2},{8,12},{10,14},{12,8},{14,10},{16,20},{18,... | collective-permute-start | bytes 208904 | tf_op jit(solution)/shard_map/ppermute | solution.py:576
  199.4 4.1 %collective-permute-start.19 = (bf16[16,2176]{1,0:T(8,128)(2,1)S(1)}, bf16[16,2176]{1,0:T(8,128)(2,1)S(1)}, u32[]{:S(2)}, u32[]{:S(2)}) collective-permute-start(bf16[16,2176]{1,0:T(8,128)(2,1)S(1)} %add_convert_fusion.1.refs_0_), channel_id=1, source_target_pairs={{0,6},{2,4},{4,2},{6,0},{8,14},{10,12},{12,10},{14,8},{16,22},{18,... | collective-permute-start | bytes 208904 | tf_op jit(solution)/shard_map/ppermute | solution.py:576
  (12 other events, 18.6 us)
where the time goes:
time: 207 us; the launch traced here: 206 us
  Pallas kernels  123 us (59%)
  starting transfers between devices  45.3 us (22%)
  waiting for transfers between devices  25.3 us (12%)
  local copies, waits for them, and re-layouts  8.04 us (4%)
  matrix products  2.9 us (1%)
    pallas_call x3, Pallas kernels, attention_chunk(): pl.pallas_call(functools.partial(attention_kernel, carried is None, first...  119 us
    ppermute x7, waiting for transfers between devices, exchange(): lax.ppermute(value, 'ctx', [(i, i ^ distance) for i in range(devices)])  13.2 us
    ppermute x3, starting transfers between devices, per_device(): evens.append(lax.ppermute(own, 'ctx', even_two))  12.8 us
    ppermute x7, starting transfers between devices, exchange(): lax.ppermute(value, 'ctx', [(i, i ^ distance) for i in range(devices)])  9.28 us
    ppermute x3, starting transfers between devices, per_device(): odd = lax.ppermute(one, 'ctx', even_one)  8.42 us
    ppermute x3, starting transfers between devices, per_device(): ones.append(lax.ppermute(own, 'ctx', forward_one))  7.72 us
    unnamed x48, local copies, waits for them, and re-layouts  7.26 us
    ppermute x2, starting transfers between devices, head_sum(): other = lax.ppermute(x, 'head', [(0, 1), (1, 0)])  4.51 us
  transfers between devices with their start and end apart: 20, of which 12 were waited for; matrix products, arithmetic and copies ran while one was open for 0% of the time, Pallas kernels for 43%

commit v1 on v0

--- a/solution.py
+++ b/solution.py
@@ -45,15 +45,21 @@
 
 
 def rotate_into(chunks, cosines, sines, key_ref, value_ref, outs):
-    own = pl.ds(0, key_ref.shape[0])
     for (first, last), out_ref in zip(chunks, outs):
         count = last - first
-        for head in range(first, last):
-            cols = pl.ds(head * HEAD_SIZE, HEAD_SIZE)
-            key = key_ref[:, cols].astype(jnp.float32)
+        own = pl.ds(0, key_ref.shape[0])
+
+        def one_head(head, carry, first=first, count=count, out_ref=out_ref, own=own):
+            def cols(at):
+                return pl.ds(pl.multiple_of(at * HEAD_SIZE, HEAD_SIZE), HEAD_SIZE)
+
+            key = key_ref[:, cols(first + head)].astype(jnp.float32)
             rotated = key * cosines + swap_halves(key) * sines
-            out_ref[own, pl.ds((head - first) * HEAD_SIZE, HEAD_SIZE)] = rotated.astype(jnp.bfloat16)
-            out_ref[own, pl.ds((count + head - first) * HEAD_SIZE, HEAD_SIZE)] = value_ref[:, cols]
+            out_ref[own, cols(head)] = rotated.astype(jnp.bfloat16)
+            out_ref[own, cols(count + head)] = value_ref[:, cols(first + head)]
+            return carry
+
+        lax.fori_loop(0, count, one_head, 0)
 
 
 def prologue_kernel(chunks, positions_ref, frequency_ref, key_ref, value_ref, cos_ref, sin_ref, *outs):
@@ -69,13 +75,27 @@
     rotate_into(chunks, cosines, sines, key_ref, value_ref, outs)
 
 
-def later_prologue_kernel(chunks, cos_ref, sin_ref, key_ref, value_ref, *outs):
+def later_prologue_kernel(chunks, mask_ref, cos_ref, sin_ref, key_ref, value_ref, extra_ref, *outs):
     rotate_into(chunks, cos_ref[...], sin_ref[...], key_ref, value_ref, outs)
-
-
-def attention_kernel(first, start, up_columns, place_ref, *refs):
-    if first:
-        mask_ref, *refs = refs
+    tokens = key_ref.shape[0]
+    first_block = lax.axis_index("ctx") * (tokens // BLOCK)
+    reach = WINDOW // BLOCK
+    lane = lax.broadcasted_iota(jnp.int32, (BLOCK, LANES), 1)
+    for key_block in range(extra_ref.shape[0] // BLOCK):
+        extra = jnp.where(lane == OFFSET_LANE, 1.0, 0.0)
+        exists = first_block + (key_block - reach) >= 0
+        for block in range(tokens // BLOCK):
+            offset = reach + block - key_block
+            if 0 <= offset <= reach:
+                hit = (mask_ref[offset, first_block + block] == 1) & exists
+                term = jnp.where(hit, 0.0, FORBIDDEN)
+            else:
+                term = FORBIDDEN
+            extra = jnp.where(lane == block, term, extra)
+        extra_ref[key_block * BLOCK : (key_block + 1) * BLOCK, :] = extra.astype(jnp.bfloat16)
+
+
+def attention_kernel(first, start, up_columns, *refs):
     (
         query_hbm,
         gradient_hbm,
@@ -85,17 +105,17 @@
         odd_hbm,
         query_up_ref,
         value_up_ref,
-        query_low_ref,
         query_low_t_ref,
         cos_ref,
         sin_ref,
+        key_extra_hbm,
         *refs,
     ) = refs
     if not first:
-        key_extra_hbm, value_extra_hbm, _, _, back_in, *refs = refs
+        value_extra_hbm, _, _, back_in, *refs = refs
     out_hbm, partial_hbm, back_ref, *refs = refs
     if first:
-        key_extra_hbm, value_extra_hbm, *refs = refs
+        value_extra_hbm, *refs = refs
     (
         query_in,
         gradient_in,
@@ -121,7 +141,7 @@
     tiles = keys // SUB
     step_tiles = KEYS // SUB
     rows = GROUPS * SUB
-    odd = place_ref[1] == 1
+    odd = lax.axis_index("ctx") % 2 == 1
 
     def copy(source, target, sem):
         return pltpu.make_async_copy(source, target, sem)
@@ -166,7 +186,7 @@
                 copy(one_hbm.at[own_rows, cols], buf.at[head, pl.ds(tokens, tokens), main], sem.at[1]),
                 copy(own_hbm.at[own_rows, cols], buf.at[head, pl.ds(2 * tokens, tokens), main], sem.at[2]),
             ]
-            if not first:
+            if kind == 0 or not first:
                 extra_hbm = (key_extra_hbm, value_extra_hbm)[kind]
                 copies.append(copy(extra_hbm, buf.at[head, :, pl.ds(HEAD_SIZE, LANES)], sem.at[3]))
             for later in copies[1:]:
@@ -174,24 +194,6 @@
         wide_copy(gradient_hbm, gradient_in, head, 1).start()
 
     if first:
-        first_block = place_ref[0] * (tokens // BLOCK)
-        reach = WINDOW // BLOCK
-        block_lane = lax.broadcasted_iota(jnp.int32, (BLOCK, LANES), 1)
-        for key_block in range(keys // BLOCK):
-            extra = jnp.where(block_lane == OFFSET_LANE, 1.0, 0.0)
-            exists = first_block + (key_block - reach) >= 0
-            for block in range(tokens // BLOCK):
-                offset = reach + block - key_block
-                if 0 <= offset <= reach:
-                    hit = (mask_ref[offset, first_block + block] == 1) & exists
-                    term = jnp.where(hit, 0.0, FORBIDDEN)
-                else:
-                    term = FORBIDDEN
-                extra = jnp.where(block_lane == block, term, extra)
-            for head in range(heads):
-                key_buf[head, key_block * BLOCK : (key_block + 1) * BLOCK, HEAD_SIZE:] = extra.astype(
-                    jnp.bfloat16
-                )
         for low_copy in low_copies:
             low_copy.wait()
         low = jnp.concatenate([low_buf[at] for at in range(3)], axis=1)
@@ -206,10 +208,7 @@
         low = jnp.transpose(low).astype(jnp.bfloat16)
         for head in range(heads):
             value_buf[head, :, HEAD_SIZE:] = low
-        extras = (
-            copy(key_buf.at[0, :, pl.ds(HEAD_SIZE, LANES)], key_extra_hbm, sems.at[6]),
-            copy(value_buf.at[0, :, pl.ds(HEAD_SIZE, LANES)], value_extra_hbm, sems.at[7]),
-        )
+        extras = (copy(value_buf.at[0, :, pl.ds(HEAD_SIZE, LANES)], value_extra_hbm, sems.at[7]),)
         for extra_copy in extras:
             extra_copy.start()
         back_ref[...] = jnp.zeros_like(back_ref)
@@ -261,7 +260,7 @@
         for step in range(steps):
             cosines = cos_ref[own(step), :]
             sines = sin_ref[own(step), :]
-            adapted = mm(query_low_ref[own(step), :], query_up_ref[start + head])
+            adapted = mm(query_low_t_ref[:, own(step)], query_up_ref[start + head], BOTH_MAJOR)
             turned = []
             for member in range(GROUPS):
                 part = query_in[head, own(step), member_cols(member)].astype(jnp.float32)
@@ -410,7 +409,7 @@
             copy(
                 source, buf.at[head, pl.ds(part * tokens, tokens), main], head_sems.at[head, kind, part]
             ).wait()
-        if not first:
+        if kind == 0 or not first:
             extra_hbm = (key_extra_hbm, value_extra_hbm)[kind]
             copy(
                 extra_hbm, buf.at[head, :, pl.ds(HEAD_SIZE, LANES)], head_sems.at[head, kind, 3]
@@ -470,7 +469,7 @@
 
 
 def attention_chunk(
-    first, last, together, columns, place, mask, query_base, gradient, received, shared, tables, carried
+    first, last, together, columns, query_base, gradient, received, shared, tables, carried
 ):
     count = last - first
     tokens = query_base.shape[0]
@@ -482,19 +481,15 @@
         jax.ShapeDtypeStruct((RANK, columns), jnp.bfloat16),
         jax.ShapeDtypeStruct((RANK + keys // tokens * RANK, tokens), jnp.float32),
     ]
-    arguments = [place]
-    in_specs = [SMEM]
     if carried is None:
-        arguments.append(mask)
-        in_specs.append(SMEM)
-        out_specs += [ANY, ANY]
-        out_shape += [jax.ShapeDtypeStruct((keys, LANES), jnp.bfloat16)] * 2
-    arguments += [query_base, gradient, *received, *shared]
-    in_specs += [ANY] * 6 + [VMEM] * len(shared)
+        out_specs.append(ANY)
+        out_shape.append(jax.ShapeDtypeStruct((keys, LANES), jnp.bfloat16))
+    arguments = [query_base, gradient, *received, *shared, *tables]
+    in_specs = [ANY] * 6 + [VMEM] * len(shared) + [ANY] * len(tables)
     aliases = {}
     if carried is not None:
-        arguments += [*tables, *carried]
-        in_specs += [ANY, ANY, ANY, ANY, VMEM]
+        arguments += carried
+        in_specs += [ANY, ANY, VMEM]
         aliases = {len(arguments) - 3: 0, len(arguments) - 2: 1}
     wide_buf = HEAD_SIZE + LANES
     return pl.pallas_call(
@@ -520,7 +515,7 @@
         ],
         out_shape=out_shape,
         input_output_aliases=aliases,
-        compiler_params=pltpu.CompilerParams(vmem_limit_bytes=50 * 2**20),
+        compiler_params=pltpu.CompilerParams(vmem_limit_bytes=40 * 2**20),
     )(*arguments)
 
 
@@ -544,12 +539,13 @@
         each.wait()
 
 
-def final_kernel(scale, place_ref, *refs):
+def final_kernel(scale, *refs):
+    place = lax.axis_index("ctx") % NEAR
     gathered = [ref[...].astype(jnp.float32) * scale for ref in refs[:NEAR]]
     query_up_ref, value_up_ref, query_down_ref, value_down_ref = refs[NEAR:]
     parts = []
     for at in range(NEAR):
-        distance = (at % 2 * 2 + at // 2) ^ place_ref[0]
+        distance = (at % 2 * 2 + at // 2) ^ place
         part = gathered[0]
         for other in range(1, NEAR):
             part = jnp.where(distance == other, gathered[other], part)
@@ -588,8 +584,11 @@
     x = halve(x, place // 2, 2)
     distance = NEAR
     while distance < devices:
-        x = add(x, exchange(x, distance))
-        distance *= 2
+        radix = 4 if distance * 4 <= devices else 2
+        others = [exchange(x, distance * part) for part in range(1, radix)]
+        x = sum([other.astype(jnp.float32) for other in others], x.astype(jnp.float32))
+        x = x.astype(jnp.bfloat16)
+        distance *= radix
     return [x] + [exchange(x, distance) for distance in range(1, NEAR)]
 
 
@@ -612,7 +611,6 @@
 ):
     tokens = hidden_states.shape[0]
     devices = lax.axis_size("ctx")
-    device_index = lax.axis_index("ctx")
     kv_heads = key_base.shape[1] // HEAD_SIZE
     forward_one = [(i, i + 1) for i in range(devices - 1)]
     even_two = [(i, i + 2) for i in range(0, devices - 2, 2)]
@@ -635,20 +633,23 @@
     cosines, sines, packed_first = pl.pallas_call(
         functools.partial(prologue_kernel, CHUNKS[:1]),
         out_shape=[table, table, payload(CHUNKS[0])],
-        compiler_params=pltpu.CompilerParams(vmem_limit_bytes=32 * 2**20),
+        compiler_params=pltpu.CompilerParams(vmem_limit_bytes=16 * 2**20),
     )(positions[None, :], jnp.asarray(frequency), key_base, frozen_value_rows)
     packed_first = lax.dynamic_update_slice(packed_first, value_low_t, (tokens, 0))
-    packed_later = pl.pallas_call(
+    key_extra, *packed_later = pl.pallas_call(
         functools.partial(later_prologue_kernel, CHUNKS[1:]),
-        out_shape=[payload(chunk) for chunk in CHUNKS[1:]],
-        compiler_params=pltpu.CompilerParams(vmem_limit_bytes=32 * 2**20),
-    )(cosines, after(sines, packed_first), key_base, frozen_value_rows)
+        in_specs=[SMEM] + [VMEM] * 4,
+        out_shape=[
+            jax.ShapeDtypeStruct((3 * tokens, LANES), jnp.bfloat16),
+            *(payload(chunk) for chunk in CHUNKS[1:]),
+        ],
+        compiler_params=pltpu.CompilerParams(vmem_limit_bytes=16 * 2**20),
+    )(block_mask.T, cosines, after(sines, packed_first), key_base, frozen_value_rows)
     packed = [packed_first, *packed_later]
 
-    place = jnp.stack([device_index, device_index % 2]).astype(jnp.int32)
     query_ups = query_up.reshape(RANK, kv_heads, GROUP_WIDTH).transpose(1, 0, 2)
     value_ups = value_up_weight.reshape(RANK, kv_heads, HEAD_SIZE).transpose(1, 0, 2)
-    shared = [query_ups, value_ups, query_low_t.T, query_low_t, cosines, sines]
+    shared = [query_ups, value_ups, query_low_t, cosines, sines]
 
     ones, evens = [], []
     for chunk, own in enumerate(packed):
@@ -663,18 +664,16 @@
     columns = query_columns + value_columns + 2 * features
     columns = -(-columns // (NEAR * LANES)) * NEAR * LANES
     carried = None
-    tables = None
+    tables = [key_extra]
     for chunk, (first, last) in enumerate(CHUNKS):
         one = ones[chunk]
-        one = after(one, evens[0] if carried is None else carried[2])
+        one = after(one, evens[chunk], *([] if carried is None else [carried[2]]))
         odd = lax.ppermute(one, "ctx", even_one)
         *carried, = attention_chunk(
             first,
             last,
             TOGETHER[chunk],
             columns,
-            place,
-            block_mask.T,
             query_base,
             output_gradient,
             [packed[chunk], one, evens[chunk], odd],
@@ -682,9 +681,8 @@
             tables,
             carried,
         )
-        if tables is None:
-            tables = carried[3:]
-            carried = carried[:3]
+        tables = tables + carried[3:]
+        carried = carried[:3]
     attention_out, partial, back = carried
 
     back = head_sum(back.astype(jnp.bfloat16))
@@ -703,16 +701,16 @@
             pltpu.SemaphoreType.DMA((2,)),
         ],
         input_output_aliases={len(arguments) - 1: 0},
-        compiler_params=pltpu.CompilerParams(vmem_limit_bytes=32 * 2**20),
+        compiler_params=pltpu.CompilerParams(vmem_limit_bytes=16 * 2**20),
     )(*arguments)
     gathered = ctx_sum(partial)
     widths = (query_columns, value_columns, features, features)
     up_query, up_value, down_query, down_value = pl.pallas_call(
         functools.partial(final_kernel, float((devices * tokens) ** (-0.5))),
-        in_specs=[SMEM] + [VMEM] * NEAR,
+        in_specs=[VMEM] * NEAR,
         out_specs=[VMEM] * 4,
         out_shape=[jax.ShapeDtypeStruct((RANK, width), jnp.float32) for width in widths],
-    )((device_index % NEAR).astype(jnp.int32).reshape(1), *gathered)
+    )(*gathered)
     return attention_out, down_query.T, up_query, down_value.T, up_value
 
 

time: 207 us -> 198 us (0.957)
  local copies, waits for them, and re-layouts: 8.04 us -> 0.75 us
  starting transfers between devices: 45.3 us -> 47.4 us
    unnamed x48 -> x28, local copies, waits for them, and re-layouts: 7.26 us -> 0.69 us
    ppermute x3, starting transfers between devices: 8.42 us -> 11.9 us  [per_device(): odd = lax.ppermute(one, 'ctx', even_one)]
    pallas_call x3, Pallas kernels: 119 us -> 116 us  [attention_chunk(): pl.pallas_call(functools.partial(attention_kernel, carried is None, first...]
    ppermute x7 -> x8, starting transfers between devices: 9.28 us -> 10.5 us  [exchange(): lax.ppermute(value, 'ctx', [(i, i ^ distance) for i in range(devices)])]
    ppermute x7 -> x8, waiting for transfers between devices: 13.2 us -> 13 us  [exchange(): lax.ppermute(value, 'ctx', [(i, i ^ distance) for i in range(devices)])]
  transfers between devices with their start and end apart: 20 -> 21, of which waited for: 12 -> 11; matrix products, arithmetic and copies ran while one was open for 0% -> 0% of each run, Pallas kernels for 43% -> 45%
where the time goes in v1:
time: 198 us
  Pallas kernels  122 us (62%)
  starting transfers between devices  47.4 us (24%)
  waiting for transfers between devices  24.2 us (12%)
  matrix products  2.9 us (1%)
    pallas_call x3, Pallas kernels, attention_chunk(): pl.pallas_call(functools.partial(attention_kernel, carried is None, first...  116 us
    ppermute x8, waiting for transfers between devices, exchange(): lax.ppermute(value, 'ctx', [(i, i ^ distance) for i in range(devices)])  13 us
    ppermute x3, starting transfers between devices, per_device(): odd = lax.ppermute(one, 'ctx', even_one)  11.9 us
    ppermute x3, starting transfers between devices, per_device(): evens.append(lax.ppermute(own, 'ctx', even_two))  11.1 us
    ppermute x8, starting transfers between devices, exchange(): lax.ppermute(value, 'ctx', [(i, i ^ distance) for i in range(devices)])  10.5 us
    ppermute x3, starting transfers between devices, per_device(): ones.append(lax.ppermute(own, 'ctx', forward_one))  6.81 us
    ppermute x2, starting transfers between devices, head_sum(): other = lax.ppermute(x, 'head', [(0, 1), (1, 0)])  4.56 us
    ppermute x2, waiting for transfers between devices, head_sum(): other = lax.ppermute(x, 'head', [(0, 1), (1, 0)])  3.98 us
  transfers between devices with their start and end apart: 21, of which 11 were waited for; matrix products, arithmetic and copies ran while one was open for 0% of the time, Pallas kernels for 45%

profile of v1, /device:TPU:0, one launch (start us, length us, event | category | flops | bytes accessed | tf_op | source)
XLA Modules:
  0.0 198.1 jit_solution(3973754845579388650)
XLA Ops:
  0.7 2.9 %fusion = f32[32,512]{1,0:T(8,128)S(1)} fusion(bf16[512,2688]{1,0:T(8,128)(2,1)} %hidden_ref.1, bf16[2688,16]{0,1:T(8,128)(2,1)} %param.18, bf16[2688,16]{0,1:T(8,128)(2,1)} %param.16), kind=kOutput, calls=%fused_computation.1 | convolution fusion | flops 88424448 | bytes 2990080 | tf_op jit(solution)/shard_map/dot_general | solution.py:40
  3.6 3.0 %collective-permute-start = (f32[32,512]{1,0:T(8,128)S(1)}, f32[32,512]{1,0:T(8,128)S(1)}, u32[]{:S(2)}, u32[]{:S(2)}) collective-permute-start(f32[32,512]{1,0:T(8,128)S(1)} %fusion), channel_id=1, source_target_pairs={{0,1},{1,0},{2,3},{3,2},{4,5},{5,4},{6,7},{7,6},{8,9},{9,8},{10,11... | collective-permute-start | bytes 196616 | tf_op jit(solution)/shard_map/ppermute | solution.py:562
  7.7 1.1 collective-permute-done
  8.8 4.0 %collective-permute-start.2 = (bf16[528,512]{1,0:T(8,128)(2,1)S(1)}, bf16[528,512]{1,0:T(8,128)(2,1)S(1)}, u32[]{:S(2)}, u32[]{:S(2)}) collective-permute-start(bf16[528,512]{1,0:T(8,128)(2,1)S(1)} %get-tuple-element.58.refs_2_), channel_id=1, source_target_pairs={{0,4},{4,8},{8,12},{12,16},{16,20},{20,24},{24,28},{1,5},{5,9},{9,... | collective-permute-start | bytes 1622024 | tf_op jit(solution)/shard_map/ppermute | solution.py:659
  12.8 1.3 collective-permute-start.6
  14.2 1.9 shard_map.156
  16.1 4.2 %collective-permute-start.1 = (bf16[512,1024]{1,0:T(8,128)(2,1)S(1)}, bf16[512,1024]{1,0:T(8,128)(2,1)S(1)}, u32[]{:S(2)}, u32[]{:S(2)}) collective-permute-start(bf16[512,1024]{1,0:T(8,128)(2,1)S(1)} %get-tuple-element.35.refs_2_), channel_id=1, source_target_pairs={{0,2},{2,4},{4,6},{6,8},{8,10},{10,12},{12,14},{14,16},{16,18},{18... | collective-permute-start | bytes 3145736 | tf_op jit(solution)/shard_map/ppermute | solution.py:658
  20.2 3.4 %collective-permute-start.5 = (bf16[512,1024]{1,0:T(8,128)(2,1)S(1)}, bf16[512,1024]{1,0:T(8,128)(2,1)S(1)}, u32[]{:S(2)}, u32[]{:S(2)}) collective-permute-start(bf16[512,1024]{1,0:T(8,128)(2,1)S(1)} %get-tuple-element.35.refs_2_), channel_id=1, source_target_pairs={{0,4},{4,8},{8,12},{12,16},{16,20},{20,24},{24,28},{1,5},{5,9},{9,... | collective-permute-start | bytes 3145736 | tf_op jit(solution)/shard_map/ppermute | solution.py:659
  23.7 4.5 %collective-permute-start.7 = (bf16[528,512]{1,0:T(8,128)(2,1)S(1)}, bf16[528,512]{1,0:T(8,128)(2,1)S(1)}, u32[]{:S(2)}, u32[]{:S(2)}) collective-permute-start(bf16[528,512]{1,0:T(8,128)(2,1)S(1)} %collective-permute-done.6.refs_3_), channel_id=1, source_target_pairs={{0,2},{4,6},{8,10},{12,14},{16,18},{20,22},{24,26},{28,30},{1,3},{... | collective-permute-start | bytes 1622024 | tf_op jit(solution)/shard_map/ppermute | solution.py:671
  28.2 1.5 collective-permute-done.7.refs_5_
  29.7 29.0 %shard_map.157 = (bf16[512,2048]{1,0:T(8,128)(2,1)}, bf16[16,8704]{1,0:T(8,128)(2,1)S(1)}, f32[64,512]{1,0:T(8,128)S(1)}, bf16[1536,128]{1,0:T(8,128)(2,1)S(1)}) custom-call(bf16[512,2048]{1,0:T(8,128)(2,1)S(1)} %copy-done.1, bf16[512,2048]{1,0:T(8,128)(2,1)S(1)} %copy-done.2, bf16[528,512]{1,0:T(8,128)(2,1)S(1)} %get-tuple-element.58.refs_2_, ...), custom_call_target="tpu_custom_call" | custom-call | tf_op jit(solution)/shard_map/pallas_call | solution.py:495
  58.7 2.3 %collective-permute-start.8 = (bf16[512,1024]{1,0:T(8,128)(2,1)S(1)}, bf16[512,1024]{1,0:T(8,128)(2,1)S(1)}, u32[]{:S(2)}, u32[]{:S(2)}) collective-permute-start(bf16[512,1024]{1,0:T(8,128)(2,1)S(1)} %collective-permute-done.1.refs_3_), channel_id=1, source_target_pairs={{0,2},{4,6},{8,10},{12,14},{16,18},{20,22},{24,26},{28,30},{1,3},{... | collective-permute-start | bytes 3145736 | tf_op jit(solution)/shard_map/ppermute | solution.py:671
  61.1 3.7 %collective-permute-start.4 = (bf16[512,512]{1,0:T(8,128)(2,1)S(1)}, bf16[512,512]{1,0:T(8,128)(2,1)S(1)}, u32[]{:S(2)}, u32[]{:S(2)}) collective-permute-start(bf16[512,512]{1,0:T(8,128)(2,1)S(1)} %get-tuple-element.36.refs_2_), channel_id=1, source_target_pairs={{0,4},{4,8},{8,12},{12,16},{16,20},{20,24},{24,28},{1,5},{5,9},{9,... | collective-permute-start | bytes 1572872 | tf_op jit(solution)/shard_map/ppermute | solution.py:659
  64.8 1.3 collective-permute-start.3
  66.1 57.0 %shard_map.158 = (bf16[512,2048]{1,0:T(8,128)(2,1)}, bf16[16,8704]{1,0:T(8,128)(2,1)S(1)}, f32[64,512]{1,0:T(8,128)S(1)}) custom-call(bf16[512,2048]{1,0:T(8,128)(2,1)S(1)} %copy-done.1, bf16[512,2048]{1,0:T(8,128)(2,1)S(1)} %copy-done.2, bf16[512,1024]{1,0:T(8,128)(2,1)S(1)} %get-tuple-element.35.refs_2_, ...), custom_call_target="tpu_custom_call", output_to_operand_aliasing={{0}: (13, {}), {1}: (14, {})} | custom-call | tf_op jit(solution)/shard_map/pallas_call | solution.py:495
  123.1 5.0 %collective-permute-start.9 = (bf16[512,512]{1,0:T(8,128)(2,1)S(1)}, bf16[512,512]{1,0:T(8,128)(2,1)S(1)}, u32[]{:S(2)}, u32[]{:S(2)}) collective-permute-start(bf16[512,512]{1,0:T(8,128)(2,1)S(1)} %collective-permute-done.3.refs_3_), channel_id=1, source_target_pairs={{0,2},{4,6},{8,10},{12,14},{16,18},{20,22},{24,26},{28,30},{1,3},{... | collective-permute-start | bytes 1572872 | tf_op jit(solution)/shard_map/ppermute | solution.py:671
  128.1 1.5 collective-permute-done.9.refs_5_
  129.6 30.2 %shard_map.159 = (bf16[512,2048]{1,0:T(8,128)(2,1)}, bf16[16,8704]{1,0:T(8,128)(2,1)S(1)}, f32[64,512]{1,0:T(8,128)S(1)}) custom-call(bf16[512,2048]{1,0:T(8,128)(2,1)S(1)} %copy-done.1, bf16[512,2048]{1,0:T(8,128)(2,1)S(1)} %copy-done.2, bf16[512,512]{1,0:T(8,128)(2,1)S(1)} %get-tuple-element.36.refs_2_, ...), custom_call_target="tpu_custom_call", output_to_operand_aliasing={{0}: (13, {}), {1}: (14, {})} | custom-call | tf_op jit(solution)/shard_map/pallas_call | solution.py:495
  159.8 1.6 collective-permute-start.10
  161.5 2.8 %collective-permute-done.10 = bf16[64,512]{1,0:T(8,128)(2,1)S(1)} collective-permute-done((bf16[64,512]{1,0:T(8,128)(2,1)S(1)}, bf16[64,512]{1,0:T(8,128)(2,1)S(1)}, u32[]{:S(2)}, u32[]{:S(2)}) %collective-permute-start.10) | collective-permute-done | bytes 65568 | tf_op jit(solution)/shard_map/ppermute | solution.py:562
  164.3 1.3 collective-permute-start.11
  165.6 1.3 collective-permute-start.12
  167.4 3.9 %collective-permute-done.12.two_ref = bf16[16,512]{1,0:T(8,128)(2,1)S(1)} collective-permute-done((bf16[16,512]{1,0:T(8,128)(2,1)S(1)}, bf16[16,512]{1,0:T(8,128)(2,1)S(1)}, u32[]{:S(2)}, u32[]{:S(2)}) %collective-permute-start.12) | collective-permute-done | bytes 16416 | tf_op jit(solution)/shard_map/ppermute | solution.py:692
  172.2 1.2 collective-permute-done.13
  173.5 2.8 %collective-permute-start.14 = (bf16[16,2176]{1,0:T(8,128)(2,1)S(1)}, bf16[16,2176]{1,0:T(8,128)(2,1)S(1)}, u32[]{:S(2)}, u32[]{:S(2)}) collective-permute-start(bf16[16,2176]{1,0:T(8,128)(2,1)S(1)} %constant_dynamic-slice_fusion), channel_id=1, source_target_pairs={{0,4},{2,6},{4,0},{6,2},{8,12},{10,14},{12,8},{14,10},{16,20},{18,... | collective-permute-start | bytes 208904 | tf_op jit(solution)/shard_map/ppermute | solution.py:572
  176.3 2.5 %collective-permute-done.14 = bf16[16,2176]{1,0:T(8,128)(2,1)S(1)} collective-permute-done((bf16[16,2176]{1,0:T(8,128)(2,1)S(1)}, bf16[16,2176]{1,0:T(8,128)(2,1)S(1)}, u32[]{:S(2)}, u32[]{:S(2)}) %collective-permute-start.14) | collective-permute-done | bytes 69664 | tf_op jit(solution)/shard_map/ppermute | solution.py:572
  178.8 2.4 %collective-permute-start.15 = (bf16[16,2176]{1,0:T(8,128)(2,1)S(1)}, bf16[16,2176]{1,0:T(8,128)(2,1)S(1)}, u32[]{:S(2)}, u32[]{:S(2)}) collective-permute-start(bf16[16,2176]{1,0:T(8,128)(2,1)S(1)} %add_convert_fusion.2), channel_id=1, source_target_pairs={{0,8},{2,10},{4,12},{6,14},{8,0},{10,2},{12,4},{14,6},{16,24},{18,... | collective-permute-start | bytes 208904 | tf_op jit(solution)/shard_map/ppermute | solution.py:572
  181.1 2.2 %collective-permute-start.16 = (bf16[16,2176]{1,0:T(8,128)(2,1)S(1)}, bf16[16,2176]{1,0:T(8,128)(2,1)S(1)}, u32[]{:S(2)}, u32[]{:S(2)}) collective-permute-start(bf16[16,2176]{1,0:T(8,128)(2,1)S(1)} %add_convert_fusion.2), channel_id=1, source_target_pairs={{0,16},{2,18},{4,20},{6,22},{8,24},{10,26},{12,28},{14,30},{16,0},... | collective-permute-start | bytes 208904 | tf_op jit(solution)/shard_map/ppermute | solution.py:572
  184.4 5.4 %collective-permute-done.16 = bf16[16,2176]{1,0:T(8,128)(2,1)S(1)} collective-permute-done((bf16[16,2176]{1,0:T(8,128)(2,1)S(1)}, bf16[16,2176]{1,0:T(8,128)(2,1)S(1)}, u32[]{:S(2)}, u32[]{:S(2)}) %collective-permute-start.16) | collective-permute-done | bytes 69664 | tf_op jit(solution)/shard_map/ppermute | solution.py:572
  189.9 1.3 collective-permute-start.19
  191.8 3.1 %collective-permute-done.19.refs_2_ = bf16[16,2176]{1,0:T(8,128)(2,1)S(1)} collective-permute-done((bf16[16,2176]{1,0:T(8,128)(2,1)S(1)}, bf16[16,2176]{1,0:T(8,128)(2,1)S(1)}, u32[]{:S(2)}, u32[]{:S(2)}) %collective-permute-start.19) | collective-permute-done | bytes 69664 | tf_op jit(solution)/shard_map/ppermute | solution.py:572
  196.3 1.8 shard_map.161
  (58 shorter events, 5.8 us)
Async XLA Ops:
  0.6 27.6 %copy-start = (bf16[16,1024]{1,0:T(8,128)(2,1)S(1)}, bf16[16,1024]{1,0:T(8,128)(2,1)}, u32[]{:S(2)}) copy-start(bf16[16,1024]{1,0:T(8,128)(2,1)} %param.19) | copy-start | bytes 98308
  0.6 5.9 %copy-start.6 = (f32[64,1]{1,0:T(8,128)S(1)}, f32[64,1]{1,0:T(8,128)}, u32[]{:S(2)}) copy-start(f32[64,1]{1,0:T(8,128)} %constant.52.clone.frequency_ref) | copy-start | bytes 772
  0.7 5.9 %copy-start.8 = (s32[512]{0:T(512)S(1)}, s32[512]{0:T(512)}, u32[]{:S(2)}) copy-start(s32[512]{0:T(512)} %param.20) | copy-start | bytes 6148
  0.7 5.9 %copy-start.4 = (bf16[512,1024]{1,0:T(8,128)(2,1)S(1)}, bf16[512,1024]{1,0:T(8,128)(2,1)}, u32[]{:S(2)}) copy-start(bf16[512,1024]{1,0:T(8,128)(2,1)} %key_ref.3) | copy-start | bytes 3145732
  0.7 5.9 %copy-start.5 = (bf16[512,1024]{1,0:T(8,128)(2,1)S(1)}, bf16[512,1024]{1,0:T(8,128)(2,1)}, u32[]{:S(2)}) copy-start(bf16[512,1024]{1,0:T(8,128)(2,1)} %value_ref.3) | copy-start | bytes 3145732
  0.7 13.5 %copy-start.7 = (s32[64,9]{0,1:T(8,128)S(1)}, s32[64,9]{0,1:T(8,128)}, u32[]{:S(2)}) copy-start(s32[64,9]{0,1:T(8,128)} %param.21) | copy-start | bytes 6916
  3.6 5.2 %collective-permute-start = (f32[32,512]{1,0:T(8,128)S(1)}, f32[32,512]{1,0:T(8,128)S(1)}, u32[]{:S(2)}, u32[]{:S(2)}) collective-permute-start(f32[32,512]{1,0:T(8,128)S(1)} %fusion), channel_id=1, source_target_pairs={{0,1},{1,0},{2,3},{3,2},{4,5},{5,4},{6,7},{7,6},{8,9},{9,8},{10,11... | collective-permute-start | bytes 196616 | tf_op jit(solution)/shard_map/ppermute | solution.py:562
  6.6 21.6 %copy-start.13 = (bf16[16,2048]{1,0:T(8,128)(2,1)S(1)}, bf16[16,2048]{1,0:T(8,128)(2,1)}, u32[]{:S(2)}) copy-start(bf16[16,2048]{1,0:T(8,128)(2,1)} %param.17) | copy-start | bytes 196612
  6.6 23.1 %copy-start.1 = (bf16[512,2048]{1,0:T(8,128)(2,1)S(1)}, bf16[512,2048]{1,0:T(8,128)(2,1)}, u32[]{:S(2)}) copy-start(bf16[512,2048]{1,0:T(8,128)(2,1)} %refs_0_.5) | copy-start | bytes 6291460
  6.6 23.1 %copy-start.2 = (bf16[512,2048]{1,0:T(8,128)(2,1)S(1)}, bf16[512,2048]{1,0:T(8,128)(2,1)}, u32[]{:S(2)}) copy-start(bf16[512,2048]{1,0:T(8,128)(2,1)} %refs_1_.5) | copy-start | bytes 6291460
  8.8 14.8 %collective-permute-start.2 = (bf16[528,512]{1,0:T(8,128)(2,1)S(1)}, bf16[528,512]{1,0:T(8,128)(2,1)S(1)}, u32[]{:S(2)}, u32[]{:S(2)}) collective-permute-start(bf16[528,512]{1,0:T(8,128)(2,1)S(1)} %get-tuple-element.58.refs_2_), channel_id=1, source_target_pairs={{0,4},{4,8},{8,12},{12,16},{16,20},{20,24},{24,28},{1,5},{5,9},{9,... | collective-permute-start | bytes 1622024 | tf_op jit(solution)/shard_map/ppermute | solution.py:659
  12.8 10.9 %collective-permute-start.6 = (bf16[528,512]{1,0:T(8,128)(2,1)S(1)}, bf16[528,512]{1,0:T(8,128)(2,1)S(1)}, u32[]{:S(2)}, u32[]{:S(2)}) collective-permute-start(bf16[528,512]{1,0:T(8,128)(2,1)S(1)} %get-tuple-element.58.refs_2_), channel_id=1, source_target_pairs={{0,2},{2,4},{4,6},{6,8},{8,10},{10,12},{12,14},{14,16},{16,18},{18... | collective-permute-start | bytes 1622024 | tf_op jit(solution)/shard_map/ppermute | solution.py:658
  16.1 42.6 %collective-permute-start.1 = (bf16[512,1024]{1,0:T(8,128)(2,1)S(1)}, bf16[512,1024]{1,0:T(8,128)(2,1)S(1)}, u32[]{:S(2)}, u32[]{:S(2)}) collective-permute-start(bf16[512,1024]{1,0:T(8,128)(2,1)S(1)} %get-tuple-element.35.refs_2_), channel_id=1, source_target_pairs={{0,2},{2,4},{4,6},{6,8},{8,10},{10,12},{12,14},{14,16},{16,18},{18... | collective-permute-start | bytes 3145736 | tf_op jit(solution)/shard_map/ppermute | solution.py:658
  20.2 38.5 %collective-permute-start.5 = (bf16[512,1024]{1,0:T(8,128)(2,1)S(1)}, bf16[512,1024]{1,0:T(8,128)(2,1)S(1)}, u32[]{:S(2)}, u32[]{:S(2)}) collective-permute-start(bf16[512,1024]{1,0:T(8,128)(2,1)S(1)} %get-tuple-element.35.refs_2_), channel_id=1, source_target_pairs={{0,4},{4,8},{8,12},{12,16},{16,20},{20,24},{24,28},{1,5},{5,9},{9,... | collective-permute-start | bytes 3145736 | tf_op jit(solution)/shard_map/ppermute | solution.py:659
  23.7 6.0 %collective-permute-start.7 = (bf16[528,512]{1,0:T(8,128)(2,1)S(1)}, bf16[528,512]{1,0:T(8,128)(2,1)S(1)}, u32[]{:S(2)}, u32[]{:S(2)}) collective-permute-start(bf16[528,512]{1,0:T(8,128)(2,1)S(1)} %collective-permute-done.6.refs_3_), channel_id=1, source_target_pairs={{0,2},{4,6},{8,10},{12,14},{16,18},{20,22},{24,26},{28,30},{1,3},{... | collective-permute-start | bytes 1622024 | tf_op jit(solution)/shard_map/ppermute | solution.py:671
  58.7 7.4 %collective-permute-start.8 = (bf16[512,1024]{1,0:T(8,128)(2,1)S(1)}, bf16[512,1024]{1,0:T(8,128)(2,1)S(1)}, u32[]{:S(2)}, u32[]{:S(2)}) collective-permute-start(bf16[512,1024]{1,0:T(8,128)(2,1)S(1)} %collective-permute-done.1.refs_3_), channel_id=1, source_target_pairs={{0,2},{4,6},{8,10},{12,14},{16,18},{20,22},{24,26},{28,30},{1,3},{... | collective-permute-start | bytes 3145736 | tf_op jit(solution)/shard_map/ppermute | solution.py:671
  61.1 62.0 %collective-permute-start.4 = (bf16[512,512]{1,0:T(8,128)(2,1)S(1)}, bf16[512,512]{1,0:T(8,128)(2,1)S(1)}, u32[]{:S(2)}, u32[]{:S(2)}) collective-permute-start(bf16[512,512]{1,0:T(8,128)(2,1)S(1)} %get-tuple-element.36.refs_2_), channel_id=1, source_target_pairs={{0,4},{4,8},{8,12},{12,16},{16,20},{20,24},{24,28},{1,5},{5,9},{9,... | collective-permute-start | bytes 1572872 | tf_op jit(solution)/shard_map/ppermute | solution.py:659
  64.8 58.3 %collective-permute-start.3 = (bf16[512,512]{1,0:T(8,128)(2,1)S(1)}, bf16[512,512]{1,0:T(8,128)(2,1)S(1)}, u32[]{:S(2)}, u32[]{:S(2)}) collective-permute-start(bf16[512,512]{1,0:T(8,128)(2,1)S(1)} %get-tuple-element.36.refs_2_), channel_id=1, source_target_pairs={{0,2},{2,4},{4,6},{6,8},{8,10},{10,12},{12,14},{14,16},{16,18},{18... | collective-permute-start | bytes 1572872 | tf_op jit(solution)/shard_map/ppermute | solution.py:658
  123.1 6.5 %collective-permute-start.9 = (bf16[512,512]{1,0:T(8,128)(2,1)S(1)}, bf16[512,512]{1,0:T(8,128)(2,1)S(1)}, u32[]{:S(2)}, u32[]{:S(2)}) collective-permute-start(bf16[512,512]{1,0:T(8,128)(2,1)S(1)} %collective-permute-done.3.refs_3_), channel_id=1, source_target_pairs={{0,2},{4,6},{8,10},{12,14},{16,18},{20,22},{24,26},{28,30},{1,3},{... | collective-permute-start | bytes 1572872 | tf_op jit(solution)/shard_map/ppermute | solution.py:671
  129.6 41.6 %copy-start.3 = (bf16[512,2688]{1,0:T(8,128)(2,1)S(1)}, bf16[512,2688]{1,0:T(8,128)(2,1)}, u32[]{:S(2)}) copy-start(bf16[512,2688]{1,0:T(8,128)(2,1)} %hidden_ref.1) | copy-start | bytes 8257540
  159.8 4.4 %collective-permute-start.10 = (bf16[64,512]{1,0:T(8,128)(2,1)S(1)}, bf16[64,512]{1,0:T(8,128)(2,1)S(1)}, u32[]{:S(2)}, u32[]{:S(2)}) collective-permute-start(bf16[64,512]{1,0:T(8,128)(2,1)S(1)} %convert_element_type.49), channel_id=1, source_target_pairs={{0,1},{1,0},{2,3},{3,2},{4,5},{5,4},{6,7},{7,6},{8,9},{9,8},{10,11... | collective-permute-start | bytes 196616 | tf_op jit(solution)/shard_map/ppermute | solution.py:562
  164.3 3.1 %collective-permute-start.11 = (bf16[16,512]{1,0:T(8,128)(2,1)S(1)}, bf16[16,512]{1,0:T(8,128)(2,1)S(1)}, u32[]{:S(2)}, u32[]{:S(2)}) collective-permute-start(bf16[16,512]{1,0:T(8,128)(2,1)S(1)} %get-tuple-element.56), channel_id=1, source_target_pairs={{2,0},{4,2},{6,4},{8,6},{10,8},{12,10},{14,12},{16,14},{18,16},{20... | collective-permute-start | bytes 49160 | tf_op jit(solution)/shard_map/ppermute | solution.py:689
  165.6 5.6 %collective-permute-start.12 = (bf16[16,512]{1,0:T(8,128)(2,1)S(1)}, bf16[16,512]{1,0:T(8,128)(2,1)S(1)}, u32[]{:S(2)}, u32[]{:S(2)}) collective-permute-start(bf16[16,512]{1,0:T(8,128)(2,1)S(1)} %get-tuple-element.55), channel_id=1, source_target_pairs={{4,0},{6,2},{8,4},{10,6},{12,8},{14,10},{16,12},{18,14},{20,16},{2... | collective-permute-start | bytes 49160 | tf_op jit(solution)/shard_map/ppermute | solution.py:692
  172.0 1.4 collective-permute-start.13
  173.5 5.2 %collective-permute-start.14 = (bf16[16,2176]{1,0:T(8,128)(2,1)S(1)}, bf16[16,2176]{1,0:T(8,128)(2,1)S(1)}, u32[]{:S(2)}, u32[]{:S(2)}) collective-permute-start(bf16[16,2176]{1,0:T(8,128)(2,1)S(1)} %constant_dynamic-slice_fusion), channel_id=1, source_target_pairs={{0,4},{2,6},{4,0},{6,2},{8,12},{10,14},{12,8},{14,10},{16,20},{18,... | collective-permute-start | bytes 208904 | tf_op jit(solution)/shard_map/ppermute | solution.py:572
  178.8 5.6 %collective-permute-start.15 = (bf16[16,2176]{1,0:T(8,128)(2,1)S(1)}, bf16[16,2176]{1,0:T(8,128)(2,1)S(1)}, u32[]{:S(2)}, u32[]{:S(2)}) collective-permute-start(bf16[16,2176]{1,0:T(8,128)(2,1)S(1)} %add_convert_fusion.2), channel_id=1, source_target_pairs={{0,8},{2,10},{4,12},{6,14},{8,0},{10,2},{12,4},{14,6},{16,24},{18,... | collective-permute-start | bytes 208904 | tf_op jit(solution)/shard_map/ppermute | solution.py:572
  181.1 8.6 %collective-permute-start.16 = (bf16[16,2176]{1,0:T(8,128)(2,1)S(1)}, bf16[16,2176]{1,0:T(8,128)(2,1)S(1)}, u32[]{:S(2)}, u32[]{:S(2)}) collective-permute-start(bf16[16,2176]{1,0:T(8,128)(2,1)S(1)} %add_convert_fusion.2), channel_id=1, source_target_pairs={{0,16},{2,18},{4,20},{6,22},{8,24},{10,26},{12,28},{14,30},{16,0},... | collective-permute-start | bytes 208904 | tf_op jit(solution)/shard_map/ppermute | solution.py:572
  183.3 6.5 %collective-permute-start.17 = (bf16[16,2176]{1,0:T(8,128)(2,1)S(1)}, bf16[16,2176]{1,0:T(8,128)(2,1)S(1)}, u32[]{:S(2)}, u32[]{:S(2)}) collective-permute-start(bf16[16,2176]{1,0:T(8,128)(2,1)S(1)} %add_convert_fusion.2), channel_id=1, source_target_pairs={{0,24},{2,26},{4,28},{6,30},{8,16},{10,18},{12,20},{14,22},{16,8},... | collective-permute-start | bytes 208904 | tf_op jit(solution)/shard_map/ppermute | solution.py:572
  189.8 5.8 %copy-start.9 = (bf16[16,2176]{1,0:T(8,128)(2,1)}, bf16[16,2176]{1,0:T(8,128)(2,1)S(1)}, u32[]{:S(2)}) copy-start(bf16[16,2176]{1,0:T(8,128)(2,1)S(1)} %add_convert_fusion.1.refs_0_) | copy-start | bytes 208900
  189.8 1.9 collective-permute-start.18
  189.9 5.0 %collective-permute-start.19 = (bf16[16,2176]{1,0:T(8,128)(2,1)S(1)}, bf16[16,2176]{1,0:T(8,128)(2,1)S(1)}, u32[]{:S(2)}, u32[]{:S(2)}) collective-permute-start(bf16[16,2176]{1,0:T(8,128)(2,1)S(1)} %add_convert_fusion.1.refs_0_), channel_id=1, source_target_pairs={{0,4},{2,6},{4,0},{6,2},{8,12},{10,14},{12,8},{14,10},{16,20},{18,... | collective-permute-start | bytes 208904 | tf_op jit(solution)/shard_map/ppermute | solution.py:572
  191.2 4.4 %collective-permute-start.20 = (bf16[16,2176]{1,0:T(8,128)(2,1)S(1)}, bf16[16,2176]{1,0:T(8,128)(2,1)S(1)}, u32[]{:S(2)}, u32[]{:S(2)}) collective-permute-start(bf16[16,2176]{1,0:T(8,128)(2,1)S(1)} %add_convert_fusion.1.refs_0_), channel_id=1, source_target_pairs={{0,6},{2,4},{4,2},{6,0},{8,14},{10,12},{12,10},{14,8},{16,22},{18,... | collective-permute-start | bytes 208904 | tf_op jit(solution)/shard_map/ppermute | solution.py:572
  (3 other events, 5.3 us)

commit v2 on v1

--- a/solution.py
+++ b/solution.py
@@ -28,8 +28,8 @@
 OFFSET_LANE = 64
 ONES_LANE = RANK
 
-CHUNKS = ((0, 2), (2, 6), (6, 8))
-TOGETHER = (2, 2, 1)
+CHUNKS = ((0, 2), (2, 5), (5, 8))
+TOGETHER = (2, 1, 1)
 
 ROWS_BY_COLS = (((1,), (0,)), ((), ()))
 BOTH_MINOR = (((1,), (1,)), ((), ()))
@@ -430,7 +430,7 @@
             arrive(head, 1)
             forward_products(head, slot)
 
-        @pl.when(jnp.min(product_buf[:, :, ones]) < 1e-18)
+        @pl.when(jnp.min(product_buf[:, :, ones]) < 1e-27)
         def _():
             lax.fori_loop(0, together, lambda slot, c: (repeat(group * together + slot, slot), c)[1], 0)
 

time: 198 us -> 201 us (1.015)
  transfers between devices with their start and end apart: 21 -> 21, of which waited for: 11 -> 11; matrix products, arithmetic and copies ran while one was open for 0% -> 0% of each run, Pallas kernels for 45% -> 38%
where the time goes in v2:
time: 201 us; the launch traced here: 200 us
  Pallas kernels  123 us (61%)
  starting transfers between devices  47.8 us (24%)
  waiting for transfers between devices  24.4 us (12%)
  matrix products  2.9 us (1%)
    pallas_call x3, Pallas kernels, attention_chunk(): pl.pallas_call(functools.partial(attention_kernel, carried is None, first...  118 us
    ppermute x8, waiting for transfers between devices, exchange(): lax.ppermute(value, 'ctx', [(i, i ^ distance) for i in range(devices)])  13 us
    ppermute x3, starting transfers between devices, per_device(): odd = lax.ppermute(one, 'ctx', even_one)  12.2 us
    ppermute x3, starting transfers between devices, per_device(): evens.append(lax.ppermute(own, 'ctx', even_two))  11.1 us
    ppermute x8, starting transfers between devices, exchange(): lax.ppermute(value, 'ctx', [(i, i ^ distance) for i in range(devices)])  10.5 us
    ppermute x3, starting transfers between devices, per_device(): ones.append(lax.ppermute(own, 'ctx', forward_one))  6.81 us
    ppermute x2, starting transfers between devices, head_sum(): other = lax.ppermute(x, 'head', [(0, 1), (1, 0)])  4.53 us
  transfers between devices with their start and end apart: 21, of which 11 were waited for; matrix products, arithmetic and copies ran while one was open for 0% of the time, Pallas kernels for 38%

profile of v2, /device:TPU:0, one launch (start us, length us, event | category | flops | bytes accessed | tf_op | source)
XLA Modules:
  0.0 200.3 jit_solution(9908073087899926838)
XLA Ops:
  0.7 2.9 %fusion = f32[32,512]{1,0:T(8,128)S(1)} fusion(bf16[512,2688]{1,0:T(8,128)(2,1)} %hidden_ref.1, bf16[2688,16]{0,1:T(8,128)(2,1)} %param.18, bf16[2688,16]{0,1:T(8,128)(2,1)} %param.16), kind=kOutput, calls=%fused_computation.1 | convolution fusion | flops 88424448 | bytes 2990080 | tf_op jit(solution)/shard_map/dot_general | solution.py:40
  3.6 3.0 %collective-permute-start = (f32[32,512]{1,0:T(8,128)S(1)}, f32[32,512]{1,0:T(8,128)S(1)}, u32[]{:S(2)}, u32[]{:S(2)}) collective-permute-start(f32[32,512]{1,0:T(8,128)S(1)} %fusion), channel_id=1, source_target_pairs={{0,1},{1,0},{2,3},{3,2},{4,5},{5,4},{6,7},{7,6},{8,9},{9,8},{10,11... | collective-permute-start | bytes 196616 | tf_op jit(solution)/shard_map/ppermute | solution.py:562
  7.7 1.1 collective-permute-done
  8.8 4.0 %collective-permute-start.2 = (bf16[528,512]{1,0:T(8,128)(2,1)S(1)}, bf16[528,512]{1,0:T(8,128)(2,1)S(1)}, u32[]{:S(2)}, u32[]{:S(2)}) collective-permute-start(bf16[528,512]{1,0:T(8,128)(2,1)S(1)} %get-tuple-element.58.refs_2_), channel_id=1, source_target_pairs={{0,4},{4,8},{8,12},{12,16},{16,20},{20,24},{24,28},{1,5},{5,9},{9,... | collective-permute-start | bytes 1622024 | tf_op jit(solution)/shard_map/ppermute | solution.py:659
  12.8 1.3 collective-permute-start.6
  14.2 1.8 shard_map.156
  16.0 4.1 %collective-permute-start.1 = (bf16[512,768]{1,0:T(8,128)(2,1)S(1)}, bf16[512,768]{1,0:T(8,128)(2,1)S(1)}, u32[]{:S(2)}, u32[]{:S(2)}) collective-permute-start(bf16[512,768]{1,0:T(8,128)(2,1)S(1)} %get-tuple-element.35.refs_2_), channel_id=1, source_target_pairs={{0,2},{2,4},{4,6},{6,8},{8,10},{10,12},{12,14},{14,16},{16,18},{18... | collective-permute-start | bytes 2359304 | tf_op jit(solution)/shard_map/ppermute | solution.py:658
  20.1 3.4 %collective-permute-start.5 = (bf16[512,768]{1,0:T(8,128)(2,1)S(1)}, bf16[512,768]{1,0:T(8,128)(2,1)S(1)}, u32[]{:S(2)}, u32[]{:S(2)}) collective-permute-start(bf16[512,768]{1,0:T(8,128)(2,1)S(1)} %get-tuple-element.35.refs_2_), channel_id=1, source_target_pairs={{0,4},{4,8},{8,12},{12,16},{16,20},{20,24},{24,28},{1,5},{5,9},{9,... | collective-permute-start | bytes 2359304 | tf_op jit(solution)/shard_map/ppermute | solution.py:659
  23.6 4.7 %collective-permute-start.7 = (bf16[528,512]{1,0:T(8,128)(2,1)S(1)}, bf16[528,512]{1,0:T(8,128)(2,1)S(1)}, u32[]{:S(2)}, u32[]{:S(2)}) collective-permute-start(bf16[528,512]{1,0:T(8,128)(2,1)S(1)} %collective-permute-done.6.refs_3_), channel_id=1, source_target_pairs={{0,2},{4,6},{8,10},{12,14},{16,18},{20,22},{24,26},{28,30},{1,3},{... | collective-permute-start | bytes 1622024 | tf_op jit(solution)/shard_map/ppermute | solution.py:671
  28.3 1.5 collective-permute-done.7.refs_5_
  29.8 29.0 %shard_map.157 = (bf16[512,2048]{1,0:T(8,128)(2,1)}, bf16[16,8704]{1,0:T(8,128)(2,1)S(1)}, f32[64,512]{1,0:T(8,128)S(1)}, bf16[1536,128]{1,0:T(8,128)(2,1)S(1)}) custom-call(bf16[512,2048]{1,0:T(8,128)(2,1)S(1)} %copy-done.1, bf16[512,2048]{1,0:T(8,128)(2,1)S(1)} %copy-done.2, bf16[528,512]{1,0:T(8,128)(2,1)S(1)} %get-tuple-element.58.refs_2_, ...), custom_call_target="tpu_custom_call" | custom-call | tf_op jit(solution)/shard_map/pallas_call | solution.py:495
  58.8 2.3 %collective-permute-start.8 = (bf16[512,768]{1,0:T(8,128)(2,1)S(1)}, bf16[512,768]{1,0:T(8,128)(2,1)S(1)}, u32[]{:S(2)}, u32[]{:S(2)}) collective-permute-start(bf16[512,768]{1,0:T(8,128)(2,1)S(1)} %collective-permute-done.1.refs_3_), channel_id=1, source_target_pairs={{0,2},{4,6},{8,10},{12,14},{16,18},{20,22},{24,26},{28,30},{1,3},{... | collective-permute-start | bytes 2359304 | tf_op jit(solution)/shard_map/ppermute | solution.py:671
  61.2 3.7 %collective-permute-start.4 = (bf16[512,768]{1,0:T(8,128)(2,1)S(1)}, bf16[512,768]{1,0:T(8,128)(2,1)S(1)}, u32[]{:S(2)}, u32[]{:S(2)}) collective-permute-start(bf16[512,768]{1,0:T(8,128)(2,1)S(1)} %get-tuple-element.36.refs_2_), channel_id=1, source_target_pairs={{0,4},{4,8},{8,12},{12,16},{16,20},{20,24},{24,28},{1,5},{5,9},{9,... | collective-permute-start | bytes 2359304 | tf_op jit(solution)/shard_map/ppermute | solution.py:659
  64.9 1.3 collective-permute-start.3
  66.2 44.5 %shard_map.158 = (bf16[512,2048]{1,0:T(8,128)(2,1)}, bf16[16,8704]{1,0:T(8,128)(2,1)S(1)}, f32[64,512]{1,0:T(8,128)S(1)}) custom-call(bf16[512,2048]{1,0:T(8,128)(2,1)S(1)} %copy-done.1, bf16[512,2048]{1,0:T(8,128)(2,1)S(1)} %copy-done.2, bf16[512,768]{1,0:T(8,128)(2,1)S(1)} %get-tuple-element.35.refs_2_, ...), custom_call_target="tpu_custom_call", output_to_operand_aliasing={{0}: (13, {}), {1}: (14, {})} | custom-call | tf_op jit(solution)/shard_map/pallas_call | solution.py:495
  110.8 5.2 %collective-permute-start.9 = (bf16[512,768]{1,0:T(8,128)(2,1)S(1)}, bf16[512,768]{1,0:T(8,128)(2,1)S(1)}, u32[]{:S(2)}, u32[]{:S(2)}) collective-permute-start(bf16[512,768]{1,0:T(8,128)(2,1)S(1)} %collective-permute-done.3.refs_3_), channel_id=1, source_target_pairs={{0,2},{4,6},{8,10},{12,14},{16,18},{20,22},{24,26},{28,30},{1,3},{... | collective-permute-start | bytes 2359304 | tf_op jit(solution)/shard_map/ppermute | solution.py:671
  116.0 1.6 collective-permute-done.9.refs_5_
  117.6 44.5 %shard_map.159 = (bf16[512,2048]{1,0:T(8,128)(2,1)}, bf16[16,8704]{1,0:T(8,128)(2,1)S(1)}, f32[64,512]{1,0:T(8,128)S(1)}) custom-call(bf16[512,2048]{1,0:T(8,128)(2,1)S(1)} %copy-done.1, bf16[512,2048]{1,0:T(8,128)(2,1)S(1)} %copy-done.2, bf16[512,768]{1,0:T(8,128)(2,1)S(1)} %get-tuple-element.36.refs_2_, ...), custom_call_target="tpu_custom_call", output_to_operand_aliasing={{0}: (13, {}), {1}: (14, {})} | custom-call | tf_op jit(solution)/shard_map/pallas_call | solution.py:495
  162.1 1.6 collective-permute-start.10
  163.7 2.9 %collective-permute-done.10 = bf16[64,512]{1,0:T(8,128)(2,1)S(1)} collective-permute-done((bf16[64,512]{1,0:T(8,128)(2,1)S(1)}, bf16[64,512]{1,0:T(8,128)(2,1)S(1)}, u32[]{:S(2)}, u32[]{:S(2)}) %collective-permute-start.10) | collective-permute-done | bytes 65568 | tf_op jit(solution)/shard_map/ppermute | solution.py:562
  166.6 1.3 collective-permute-start.11
  167.9 1.3 collective-permute-start.12
  169.7 3.9 %collective-permute-done.12.two_ref = bf16[16,512]{1,0:T(8,128)(2,1)S(1)} collective-permute-done((bf16[16,512]{1,0:T(8,128)(2,1)S(1)}, bf16[16,512]{1,0:T(8,128)(2,1)S(1)}, u32[]{:S(2)}, u32[]{:S(2)}) %collective-permute-start.12) | collective-permute-done | bytes 16416 | tf_op jit(solution)/shard_map/ppermute | solution.py:692
  174.5 1.2 collective-permute-done.13
  175.8 2.7 %collective-permute-start.14 = (bf16[16,2176]{1,0:T(8,128)(2,1)S(1)}, bf16[16,2176]{1,0:T(8,128)(2,1)S(1)}, u32[]{:S(2)}, u32[]{:S(2)}) collective-permute-start(bf16[16,2176]{1,0:T(8,128)(2,1)S(1)} %constant_dynamic-slice_fusion), channel_id=1, source_target_pairs={{0,4},{2,6},{4,0},{6,2},{8,12},{10,14},{12,8},{14,10},{16,20},{18,... | collective-permute-start | bytes 208904 | tf_op jit(solution)/shard_map/ppermute | solution.py:572
  178.5 2.5 %collective-permute-done.14 = bf16[16,2176]{1,0:T(8,128)(2,1)S(1)} collective-permute-done((bf16[16,2176]{1,0:T(8,128)(2,1)S(1)}, bf16[16,2176]{1,0:T(8,128)(2,1)S(1)}, u32[]{:S(2)}, u32[]{:S(2)}) %collective-permute-start.14) | collective-permute-done | bytes 69664 | tf_op jit(solution)/shard_map/ppermute | solution.py:572
  181.0 2.4 %collective-permute-start.15 = (bf16[16,2176]{1,0:T(8,128)(2,1)S(1)}, bf16[16,2176]{1,0:T(8,128)(2,1)S(1)}, u32[]{:S(2)}, u32[]{:S(2)}) collective-permute-start(bf16[16,2176]{1,0:T(8,128)(2,1)S(1)} %add_convert_fusion.2), channel_id=1, source_target_pairs={{0,8},{2,10},{4,12},{6,14},{8,0},{10,2},{12,4},{14,6},{16,24},{18,... | collective-permute-start | bytes 208904 | tf_op jit(solution)/shard_map/ppermute | solution.py:572
  183.4 2.2 %collective-permute-start.16 = (bf16[16,2176]{1,0:T(8,128)(2,1)S(1)}, bf16[16,2176]{1,0:T(8,128)(2,1)S(1)}, u32[]{:S(2)}, u32[]{:S(2)}) collective-permute-start(bf16[16,2176]{1,0:T(8,128)(2,1)S(1)} %add_convert_fusion.2), channel_id=1, source_target_pairs={{0,16},{2,18},{4,20},{6,22},{8,24},{10,26},{12,28},{14,30},{16,0},... | collective-permute-start | bytes 208904 | tf_op jit(solution)/shard_map/ppermute | solution.py:572
  186.6 5.4 %collective-permute-done.16 = bf16[16,2176]{1,0:T(8,128)(2,1)S(1)} collective-permute-done((bf16[16,2176]{1,0:T(8,128)(2,1)S(1)}, bf16[16,2176]{1,0:T(8,128)(2,1)S(1)}, u32[]{:S(2)}, u32[]{:S(2)}) %collective-permute-start.16) | collective-permute-done | bytes 69664 | tf_op jit(solution)/shard_map/ppermute | solution.py:572
  192.2 1.3 collective-permute-start.19
  194.0 3.1 %collective-permute-done.19.refs_2_ = bf16[16,2176]{1,0:T(8,128)(2,1)S(1)} collective-permute-done((bf16[16,2176]{1,0:T(8,128)(2,1)S(1)}, bf16[16,2176]{1,0:T(8,128)(2,1)S(1)}, u32[]{:S(2)}, u32[]{:S(2)}) %collective-permute-start.19) | collective-permute-done | bytes 69664 | tf_op jit(solution)/shard_map/ppermute | solution.py:572
  198.5 1.8 shard_map.161
  (58 shorter events, 5.8 us)
Async XLA Ops:
  0.6 27.7 %copy-start = (bf16[16,1024]{1,0:T(8,128)(2,1)S(1)}, bf16[16,1024]{1,0:T(8,128)(2,1)}, u32[]{:S(2)}) copy-start(bf16[16,1024]{1,0:T(8,128)(2,1)} %param.19) | copy-start | bytes 98308
  0.6 5.9 %copy-start.6 = (f32[64,1]{1,0:T(8,128)S(1)}, f32[64,1]{1,0:T(8,128)}, u32[]{:S(2)}) copy-start(f32[64,1]{1,0:T(8,128)} %constant.52.clone.frequency_ref) | copy-start | bytes 772
  0.7 5.9 %copy-start.8 = (s32[512]{0:T(512)S(1)}, s32[512]{0:T(512)}, u32[]{:S(2)}) copy-start(s32[512]{0:T(512)} %param.20) | copy-start | bytes 6148
  0.7 5.9 %copy-start.4 = (bf16[512,1024]{1,0:T(8,128)(2,1)S(1)}, bf16[512,1024]{1,0:T(8,128)(2,1)}, u32[]{:S(2)}) copy-start(bf16[512,1024]{1,0:T(8,128)(2,1)} %key_ref.3) | copy-start | bytes 3145732
  0.7 5.9 %copy-start.5 = (bf16[512,1024]{1,0:T(8,128)(2,1)S(1)}, bf16[512,1024]{1,0:T(8,128)(2,1)}, u32[]{:S(2)}) copy-start(bf16[512,1024]{1,0:T(8,128)(2,1)} %value_ref.3) | copy-start | bytes 3145732
  0.7 13.5 %copy-start.7 = (s32[64,9]{0,1:T(8,128)S(1)}, s32[64,9]{0,1:T(8,128)}, u32[]{:S(2)}) copy-start(s32[64,9]{0,1:T(8,128)} %param.21) | copy-start | bytes 6916
  3.6 5.2 %collective-permute-start = (f32[32,512]{1,0:T(8,128)S(1)}, f32[32,512]{1,0:T(8,128)S(1)}, u32[]{:S(2)}, u32[]{:S(2)}) collective-permute-start(f32[32,512]{1,0:T(8,128)S(1)} %fusion), channel_id=1, source_target_pairs={{0,1},{1,0},{2,3},{3,2},{4,5},{5,4},{6,7},{7,6},{8,9},{9,8},{10,11... | collective-permute-start | bytes 196616 | tf_op jit(solution)/shard_map/ppermute | solution.py:562
  6.6 21.7 %copy-start.13 = (bf16[16,2048]{1,0:T(8,128)(2,1)S(1)}, bf16[16,2048]{1,0:T(8,128)(2,1)}, u32[]{:S(2)}) copy-start(bf16[16,2048]{1,0:T(8,128)(2,1)} %param.17) | copy-start | bytes 196612
  6.6 23.2 %copy-start.1 = (bf16[512,2048]{1,0:T(8,128)(2,1)S(1)}, bf16[512,2048]{1,0:T(8,128)(2,1)}, u32[]{:S(2)}) copy-start(bf16[512,2048]{1,0:T(8,128)(2,1)} %refs_0_.5) | copy-start | bytes 6291460
  6.6 23.2 %copy-start.2 = (bf16[512,2048]{1,0:T(8,128)(2,1)S(1)}, bf16[512,2048]{1,0:T(8,128)(2,1)}, u32[]{:S(2)}) copy-start(bf16[512,2048]{1,0:T(8,128)(2,1)} %refs_1_.5) | copy-start | bytes 6291460
  8.8 14.7 %collective-permute-start.2 = (bf16[528,512]{1,0:T(8,128)(2,1)S(1)}, bf16[528,512]{1,0:T(8,128)(2,1)S(1)}, u32[]{:S(2)}, u32[]{:S(2)}) collective-permute-start(bf16[528,512]{1,0:T(8,128)(2,1)S(1)} %get-tuple-element.58.refs_2_), channel_id=1, source_target_pairs={{0,4},{4,8},{8,12},{12,16},{16,20},{20,24},{24,28},{1,5},{5,9},{9,... | collective-permute-start | bytes 1622024 | tf_op jit(solution)/shard_map/ppermute | solution.py:659
  12.8 10.8 %collective-permute-start.6 = (bf16[528,512]{1,0:T(8,128)(2,1)S(1)}, bf16[528,512]{1,0:T(8,128)(2,1)S(1)}, u32[]{:S(2)}, u32[]{:S(2)}) collective-permute-start(bf16[528,512]{1,0:T(8,128)(2,1)S(1)} %get-tuple-element.58.refs_2_), channel_id=1, source_target_pairs={{0,2},{2,4},{4,6},{6,8},{8,10},{10,12},{12,14},{14,16},{16,18},{18... | collective-permute-start | bytes 1622024 | tf_op jit(solution)/shard_map/ppermute | solution.py:658
  16.0 42.8 %collective-permute-start.1 = (bf16[512,768]{1,0:T(8,128)(2,1)S(1)}, bf16[512,768]{1,0:T(8,128)(2,1)S(1)}, u32[]{:S(2)}, u32[]{:S(2)}) collective-permute-start(bf16[512,768]{1,0:T(8,128)(2,1)S(1)} %get-tuple-element.35.refs_2_), channel_id=1, source_target_pairs={{0,2},{2,4},{4,6},{6,8},{8,10},{10,12},{12,14},{14,16},{16,18},{18... | collective-permute-start | bytes 2359304 | tf_op jit(solution)/shard_map/ppermute | solution.py:658
  20.1 38.7 %collective-permute-start.5 = (bf16[512,768]{1,0:T(8,128)(2,1)S(1)}, bf16[512,768]{1,0:T(8,128)(2,1)S(1)}, u32[]{:S(2)}, u32[]{:S(2)}) collective-permute-start(bf16[512,768]{1,0:T(8,128)(2,1)S(1)} %get-tuple-element.35.refs_2_), channel_id=1, source_target_pairs={{0,4},{4,8},{8,12},{12,16},{16,20},{20,24},{24,28},{1,5},{5,9},{9,... | collective-permute-start | bytes 2359304 | tf_op jit(solution)/shard_map/ppermute | solution.py:659
  23.6 6.2 %collective-permute-start.7 = (bf16[528,512]{1,0:T(8,128)(2,1)S(1)}, bf16[528,512]{1,0:T(8,128)(2,1)S(1)}, u32[]{:S(2)}, u32[]{:S(2)}) collective-permute-start(bf16[528,512]{1,0:T(8,128)(2,1)S(1)} %collective-permute-done.6.refs_3_), channel_id=1, source_target_pairs={{0,2},{4,6},{8,10},{12,14},{16,18},{20,22},{24,26},{28,30},{1,3},{... | collective-permute-start | bytes 1622024 | tf_op jit(solution)/shard_map/ppermute | solution.py:671
  58.8 7.4 %collective-permute-start.8 = (bf16[512,768]{1,0:T(8,128)(2,1)S(1)}, bf16[512,768]{1,0:T(8,128)(2,1)S(1)}, u32[]{:S(2)}, u32[]{:S(2)}) collective-permute-start(bf16[512,768]{1,0:T(8,128)(2,1)S(1)} %collective-permute-done.1.refs_3_), channel_id=1, source_target_pairs={{0,2},{4,6},{8,10},{12,14},{16,18},{20,22},{24,26},{28,30},{1,3},{... | collective-permute-start | bytes 2359304 | tf_op jit(solution)/shard_map/ppermute | solution.py:671
  61.2 49.6 %collective-permute-start.4 = (bf16[512,768]{1,0:T(8,128)(2,1)S(1)}, bf16[512,768]{1,0:T(8,128)(2,1)S(1)}, u32[]{:S(2)}, u32[]{:S(2)}) collective-permute-start(bf16[512,768]{1,0:T(8,128)(2,1)S(1)} %get-tuple-element.36.refs_2_), channel_id=1, source_target_pairs={{0,4},{4,8},{8,12},{12,16},{16,20},{20,24},{24,28},{1,5},{5,9},{9,... | collective-permute-start | bytes 2359304 | tf_op jit(solution)/shard_map/ppermute | solution.py:659
  64.9 45.9 %collective-permute-start.3 = (bf16[512,768]{1,0:T(8,128)(2,1)S(1)}, bf16[512,768]{1,0:T(8,128)(2,1)S(1)}, u32[]{:S(2)}, u32[]{:S(2)}) collective-permute-start(bf16[512,768]{1,0:T(8,128)(2,1)S(1)} %get-tuple-element.36.refs_2_), channel_id=1, source_target_pairs={{0,2},{2,4},{4,6},{6,8},{8,10},{10,12},{12,14},{14,16},{16,18},{18... | collective-permute-start | bytes 2359304 | tf_op jit(solution)/shard_map/ppermute | solution.py:658
  110.8 6.8 %collective-permute-start.9 = (bf16[512,768]{1,0:T(8,128)(2,1)S(1)}, bf16[512,768]{1,0:T(8,128)(2,1)S(1)}, u32[]{:S(2)}, u32[]{:S(2)}) collective-permute-start(bf16[512,768]{1,0:T(8,128)(2,1)S(1)} %collective-permute-done.3.refs_3_), channel_id=1, source_target_pairs={{0,2},{4,6},{8,10},{12,14},{16,18},{20,22},{24,26},{28,30},{1,3},{... | collective-permute-start | bytes 2359304 | tf_op jit(solution)/shard_map/ppermute | solution.py:671
  117.6 55.9 %copy-start.3 = (bf16[512,2688]{1,0:T(8,128)(2,1)S(1)}, bf16[512,2688]{1,0:T(8,128)(2,1)}, u32[]{:S(2)}) copy-start(bf16[512,2688]{1,0:T(8,128)(2,1)} %hidden_ref.1) | copy-start | bytes 8257540
  162.1 4.4 %collective-permute-start.10 = (bf16[64,512]{1,0:T(8,128)(2,1)S(1)}, bf16[64,512]{1,0:T(8,128)(2,1)S(1)}, u32[]{:S(2)}, u32[]{:S(2)}) collective-permute-start(bf16[64,512]{1,0:T(8,128)(2,1)S(1)} %convert_element_type.49), channel_id=1, source_target_pairs={{0,1},{1,0},{2,3},{3,2},{4,5},{5,4},{6,7},{7,6},{8,9},{9,8},{10,11... | collective-permute-start | bytes 196616 | tf_op jit(solution)/shard_map/ppermute | solution.py:562
  166.6 3.1 %collective-permute-start.11 = (bf16[16,512]{1,0:T(8,128)(2,1)S(1)}, bf16[16,512]{1,0:T(8,128)(2,1)S(1)}, u32[]{:S(2)}, u32[]{:S(2)}) collective-permute-start(bf16[16,512]{1,0:T(8,128)(2,1)S(1)} %get-tuple-element.56), channel_id=1, source_target_pairs={{2,0},{4,2},{6,4},{8,6},{10,8},{12,10},{14,12},{16,14},{18,16},{20... | collective-permute-start | bytes 49160 | tf_op jit(solution)/shard_map/ppermute | solution.py:689
  167.9 5.6 %collective-permute-start.12 = (bf16[16,512]{1,0:T(8,128)(2,1)S(1)}, bf16[16,512]{1,0:T(8,128)(2,1)S(1)}, u32[]{:S(2)}, u32[]{:S(2)}) collective-permute-start(bf16[16,512]{1,0:T(8,128)(2,1)S(1)} %get-tuple-element.55), channel_id=1, source_target_pairs={{4,0},{6,2},{8,4},{10,6},{12,8},{14,10},{16,12},{18,14},{20,16},{2... | collective-permute-start | bytes 49160 | tf_op jit(solution)/shard_map/ppermute | solution.py:692
  174.3 1.4 collective-permute-start.13
  175.8 5.2 %collective-permute-start.14 = (bf16[16,2176]{1,0:T(8,128)(2,1)S(1)}, bf16[16,2176]{1,0:T(8,128)(2,1)S(1)}, u32[]{:S(2)}, u32[]{:S(2)}) collective-permute-start(bf16[16,2176]{1,0:T(8,128)(2,1)S(1)} %constant_dynamic-slice_fusion), channel_id=1, source_target_pairs={{0,4},{2,6},{4,0},{6,2},{8,12},{10,14},{12,8},{14,10},{16,20},{18,... | collective-permute-start | bytes 208904 | tf_op jit(solution)/shard_map/ppermute | solution.py:572
  181.0 5.6 %collective-permute-start.15 = (bf16[16,2176]{1,0:T(8,128)(2,1)S(1)}, bf16[16,2176]{1,0:T(8,128)(2,1)S(1)}, u32[]{:S(2)}, u32[]{:S(2)}) collective-permute-start(bf16[16,2176]{1,0:T(8,128)(2,1)S(1)} %add_convert_fusion.2), channel_id=1, source_target_pairs={{0,8},{2,10},{4,12},{6,14},{8,0},{10,2},{12,4},{14,6},{16,24},{18,... | collective-permute-start | bytes 208904 | tf_op jit(solution)/shard_map/ppermute | solution.py:572
  183.4 8.6 %collective-permute-start.16 = (bf16[16,2176]{1,0:T(8,128)(2,1)S(1)}, bf16[16,2176]{1,0:T(8,128)(2,1)S(1)}, u32[]{:S(2)}, u32[]{:S(2)}) collective-permute-start(bf16[16,2176]{1,0:T(8,128)(2,1)S(1)} %add_convert_fusion.2), channel_id=1, source_target_pairs={{0,16},{2,18},{4,20},{6,22},{8,24},{10,26},{12,28},{14,30},{16,0},... | collective-permute-start | bytes 208904 | tf_op jit(solution)/shard_map/ppermute | solution.py:572
  185.5 6.5 %collective-permute-start.17 = (bf16[16,2176]{1,0:T(8,128)(2,1)S(1)}, bf16[16,2176]{1,0:T(8,128)(2,1)S(1)}, u32[]{:S(2)}, u32[]{:S(2)}) collective-permute-start(bf16[16,2176]{1,0:T(8,128)(2,1)S(1)} %add_convert_fusion.2), channel_id=1, source_target_pairs={{0,24},{2,26},{4,28},{6,30},{8,16},{10,18},{12,20},{14,22},{16,8},... | collective-permute-start | bytes 208904 | tf_op jit(solution)/shard_map/ppermute | solution.py:572
  192.1 5.8 %copy-start.9 = (bf16[16,2176]{1,0:T(8,128)(2,1)}, bf16[16,2176]{1,0:T(8,128)(2,1)S(1)}, u32[]{:S(2)}) copy-start(bf16[16,2176]{1,0:T(8,128)(2,1)S(1)} %add_convert_fusion.1.refs_0_) | copy-start | bytes 208900
  192.1 1.9 collective-permute-start.18
  192.2 5.0 %collective-permute-start.19 = (bf16[16,2176]{1,0:T(8,128)(2,1)S(1)}, bf16[16,2176]{1,0:T(8,128)(2,1)S(1)}, u32[]{:S(2)}, u32[]{:S(2)}) collective-permute-start(bf16[16,2176]{1,0:T(8,128)(2,1)S(1)} %add_convert_fusion.1.refs_0_), channel_id=1, source_target_pairs={{0,4},{2,6},{4,0},{6,2},{8,12},{10,14},{12,8},{14,10},{16,20},{18,... | collective-permute-start | bytes 208904 | tf_op jit(solution)/shard_map/ppermute | solution.py:572
  193.4 4.4 %collective-permute-start.20 = (bf16[16,2176]{1,0:T(8,128)(2,1)S(1)}, bf16[16,2176]{1,0:T(8,128)(2,1)S(1)}, u32[]{:S(2)}, u32[]{:S(2)}) collective-permute-start(bf16[16,2176]{1,0:T(8,128)(2,1)S(1)} %add_convert_fusion.1.refs_0_), channel_id=1, source_target_pairs={{0,6},{2,4},{4,2},{6,0},{8,14},{10,12},{12,10},{14,8},{16,22},{18,... | collective-permute-start | bytes 208904 | tf_op jit(solution)/shard_map/ppermute | solution.py:572
  (3 other events, 5.3 us)

commit v3 on v2

--- a/solution.py
+++ b/solution.py
@@ -29,7 +29,6 @@
 ONES_LANE = RANK
 
 CHUNKS = ((0, 2), (2, 5), (5, 8))
-TOGETHER = (2, 1, 1)
 
 ROWS_BY_COLS = (((1,), (0,)), ((), ()))
 BOTH_MINOR = (((1,), (1,)), ((), ()))
@@ -134,7 +133,6 @@
         head_sems,
     ) = refs
     heads = key_buf.shape[0]
-    together = query_buf.shape[0]
     tokens = query_in.shape[1]
     keys = key_buf.shape[1]
     steps = tokens // SUB
@@ -170,28 +168,33 @@
         ends = (buf.at[head], hbm.at[:, cols]) if out else (hbm.at[:, cols], buf.at[head])
         return copy(*ends, head_sems.at[head, 2, kind])
 
-    for head in range(heads):
+    def start_copies(head):
+        def cols(at):
+            return pl.ds(pl.multiple_of(at * HEAD_SIZE, HEAD_SIZE), HEAD_SIZE)
+
+        main = pl.ds(0, HEAD_SIZE)
         wide_copy(query_hbm, query_in, head, 0).start()
-        for kind, buf, at in ((0, key_buf, head), (1, value_buf, heads + head)):
-            cols = pl.ds(at * HEAD_SIZE, HEAD_SIZE)
-            main = pl.ds(0, HEAD_SIZE)
-            sem = head_sems.at[head, kind]
-            copies = [
-                start_far(
-                    even_hbm.at[own_rows, cols],
-                    odd_hbm.at[own_rows, cols],
-                    buf.at[head, pl.ds(0, tokens), main],
-                    sem.at[0],
-                ),
-                copy(one_hbm.at[own_rows, cols], buf.at[head, pl.ds(tokens, tokens), main], sem.at[1]),
-                copy(own_hbm.at[own_rows, cols], buf.at[head, pl.ds(2 * tokens, tokens), main], sem.at[2]),
-            ]
+        for kind, buf, at in ((0, key_buf, cols(head)), (1, value_buf, cols(heads + head))):
+            start_far(
+                even_hbm.at[own_rows, at],
+                odd_hbm.at[own_rows, at],
+                buf.at[head, pl.ds(0, tokens), main],
+                head_sems.at[head, kind, 0],
+            )
+            for part, source in ((1, one_hbm), (2, own_hbm)):
+                copy(
+                    source.at[own_rows, at],
+                    buf.at[head, pl.ds(part * tokens, tokens), main],
+                    head_sems.at[head, kind, part],
+                ).start()
             if kind == 0 or not first:
                 extra_hbm = (key_extra_hbm, value_extra_hbm)[kind]
-                copies.append(copy(extra_hbm, buf.at[head, :, pl.ds(HEAD_SIZE, LANES)], sem.at[3]))
-            for later in copies[1:]:
-                later.start()
+                copy(
+                    extra_hbm, buf.at[head, :, pl.ds(HEAD_SIZE, LANES)], head_sems.at[head, kind, 3]
+                ).start()
         wide_copy(gradient_hbm, gradient_in, head, 1).start()
+
+    start_copies(0)
 
     if first:
         for low_copy in low_copies:
@@ -274,24 +277,24 @@
                 lane == OFFSET_LANE, -bound, chosen
             ).astype(jnp.bfloat16)
 
-    def forward_scores(head, slot):
+    def forward_scores(head):
         for tile in range(tiles):
             low, high = tile_steps(tile)
             cols = slice(tile * SUB, (tile + 1) * SUB)
             scores = mm(
-                query_buf[slot, low * rows : high * rows, :], key_buf[head, cols, :], BOTH_MINOR
+                query_buf[head % 3, low * rows : high * rows, :], key_buf[head, cols, :], BOTH_MINOR
             )
             for step in range(low, high):
                 part = limit(step, tile, scores[(step - low) * rows : (step - low + 1) * rows, :])
-                weight_buf[slot, span(step), cols] = jnp.exp2(part).astype(jnp.bfloat16)
-
-    def forward_products(head, slot):
+                weight_buf[head % 2, span(step), cols] = jnp.exp2(part).astype(jnp.bfloat16)
+
+    def forward_products(head):
         for step in range(steps):
-            product_buf[slot, span(step), :] = mm(
-                weight_buf[slot, span(step), window(step)], value_buf[head, window(step), :]
-            )
-
-    def repeat(head, slot):
+            product_buf[head % 2, span(step), :] = mm(
+                weight_buf[head % 2, span(step), window(step)], value_buf[head, window(step), :]
+            )
+
+    def repeat(head):
         diagonal = lane - row % BLOCK
 
         def one_step(step, carry):
@@ -299,7 +302,7 @@
 
             def scores_of(tile):
                 cols = pl.ds(pl.multiple_of((step + tile) * SUB, SUB), SUB)
-                part = mm(query_buf[slot, here, :], key_buf[head, cols, :], BOTH_MINOR)
+                part = mm(query_buf[head % 3, here, :], key_buf[head, cols, :], BOTH_MINOR)
                 lowest = jnp.where(tile == 0, 1, -BLOCK)
                 highest = jnp.where(tile == step_tiles - 1, 0, BLOCK)
                 halves = []
@@ -318,20 +321,20 @@
             def again(tile, sums):
                 part, cols = scores_of(tile)
                 weights = jnp.exp2(part).astype(jnp.bfloat16)
-                weight_buf[slot, here, cols] = weights
+                weight_buf[head % 2, here, cols] = weights
                 return sums + mm(weights, value_buf[head, cols, :])
 
-            extra = query_buf[slot, here, HEAD_SIZE:].astype(jnp.float32)
-            query_buf[slot, here, HEAD_SIZE:] = jnp.where(lane == OFFSET_LANE, 0.0, extra).astype(
+            extra = query_buf[head % 3, here, HEAD_SIZE:].astype(jnp.float32)
+            query_buf[head % 3, here, HEAD_SIZE:] = jnp.where(lane == OFFSET_LANE, 0.0, extra).astype(
                 jnp.bfloat16
             )
             highest = lax.fori_loop(
                 0, step_tiles, top, jnp.full((rows, 1), FORBIDDEN, jnp.float32)
             )
-            query_buf[slot, here, HEAD_SIZE:] = jnp.where(lane == OFFSET_LANE, -highest, extra).astype(
+            query_buf[head % 3, here, HEAD_SIZE:] = jnp.where(lane == OFFSET_LANE, -highest, extra).astype(
                 jnp.bfloat16
             )
-            product_buf[slot, here, :] = lax.fori_loop(
+            product_buf[head % 2, here, :] = lax.fori_loop(
                 0, step_tiles, again, jnp.zeros((rows, HEAD_SIZE + LANES), jnp.float32)
             )
             return carry
@@ -340,7 +343,7 @@
 
     kept = {}
 
-    def finish_forward(head, slot):
+    def finish_forward(head):
         value_up = value_up_of(head)
         spreads = []
         inverses = []
@@ -350,9 +353,9 @@
                 [gradient_in[head, own(step), member_cols(member)] for member in range(GROUPS)], axis=0
             )
             gradient_low = mm(gradient, value_up, BOTH_MINOR)
-            inverse = 1.0 / product_buf[slot, span(step), ones]
-            low_part = (product_buf[slot, span(step), HEAD_SIZE:] * inverse).astype(jnp.bfloat16)
-            outputs = product_buf[slot, span(step), :HEAD_SIZE] * inverse + mm(low_part, value_up)
+            inverse = 1.0 / product_buf[head % 2, span(step), ones]
+            low_part = (product_buf[head % 2, span(step), HEAD_SIZE:] * inverse).astype(jnp.bfloat16)
+            outputs = product_buf[head % 2, span(step), :HEAD_SIZE] * inverse + mm(low_part, value_up)
             outputs = outputs.astype(jnp.bfloat16)
             for member in range(GROUPS):
                 out_buf[head, own(step), member_cols(member)] = outputs[own(member), :]
@@ -362,17 +365,17 @@
             delta_high = delta.astype(jnp.bfloat16).astype(jnp.float32)
             extra = jnp.where(lane == ONES_LANE, -delta_high, gradient_low)
             extra = jnp.where(lane == ONES_LANE + 1, delta_high - delta, extra)
-            gradient_buf[slot, span(step), :HEAD_SIZE] = gradient
-            gradient_buf[slot, span(step), HEAD_SIZE:] = extra.astype(jnp.bfloat16)
+            gradient_buf[0, span(step), :HEAD_SIZE] = gradient
+            gradient_buf[0, span(step), HEAD_SIZE:] = extra.astype(jnp.bfloat16)
             up_value += mm(low_part, gradient, BOTH_MAJOR)
             spreads.append(jnp.transpose(gradient_low * inverse)[:RANK, :].astype(jnp.bfloat16))
             inverses.append(inverse * SCORE_SCALE)
         up_value_buf[head] = up_value[:RANK, :].astype(jnp.bfloat16)
         wide_copy(out_hbm, out_buf, head, 2, out=True).start()
-        kept[slot] = jnp.concatenate(spreads, axis=1), inverses
-
-    def backward_scores(head, slot):
-        spread = kept[slot][0]
+        kept[0] = jnp.concatenate(spreads, axis=1), inverses
+
+    def backward_scores(head):
+        spread = kept[0][0]
         for tile in range(tiles):
             low, high = tile_steps(tile)
             cols = slice(tile * SUB, (tile + 1) * SUB)
@@ -380,18 +383,18 @@
             back_rows = slice(back_row, back_row + RANK)
             back_cols = slice(tile * SUB % tokens, tile * SUB % tokens + SUB)
             part = slice(low * rows, high * rows)
-            grad_weights = mm(gradient_buf[slot, part, :], value_buf[head, cols, :], BOTH_MINOR)
-            weights = weight_buf[slot, part, cols]
-            score_buf[slot, part, cols] = weights * grad_weights.astype(jnp.bfloat16)
+            grad_weights = mm(gradient_buf[0, part, :], value_buf[head, cols, :], BOTH_MINOR)
+            weights = weight_buf[head % 2, part, cols]
+            score_buf[0, part, cols] = weights * grad_weights.astype(jnp.bfloat16)
             back_ref[back_rows, back_cols] += mm(spread[:, part], weights)
 
-    def backward_products(head, slot):
+    def backward_products(head):
         query_grads = []
         for step in range(steps):
             cosines = cos_ref[own(step), :]
             sines = sin_ref[own(step), :]
-            sums = mm(score_buf[slot, span(step), window(step)], key_buf[head, window(step), :HEAD_SIZE])
-            sums = sums * kept[slot][1][step]
+            sums = mm(score_buf[0, span(step), window(step)], key_buf[head, window(step), :HEAD_SIZE])
+            sums = sums * kept[0][1][step]
             turned = []
             for member in range(GROUPS):
                 part = sums[own(member), :]
@@ -415,39 +418,70 @@
                 extra_hbm, buf.at[head, :, pl.ds(HEAD_SIZE, LANES)], head_sems.at[head, kind, 3]
             ).wait()
 
-    def arrive_and_prepare(head, slot):
+    def arrive_queries(head):
         arrive(head, 0)
         wide_copy(query_hbm, query_in, head, 0).wait()
-        prepare(head, slot)
-
-    def work(group, carry):
-        members = [(group * together + slot, slot) for slot in range(together)]
-        arrive_and_prepare(*members[0])
-        for head, slot in members:
-            forward_scores(head, slot)
-            if slot + 1 < together:
-                arrive_and_prepare(*members[slot + 1])
-            arrive(head, 1)
-            forward_products(head, slot)
-
-        @pl.when(jnp.min(product_buf[:, :, ones]) < 1e-27)
+
+    def check(head):
+        @pl.when(jnp.min(product_buf[head % 2, :, ones]) < 1e-27)
         def _():
-            lax.fori_loop(0, together, lambda slot, c: (repeat(group * together + slot, slot), c)[1], 0)
-
-        for head, slot in members:
-            wide_copy(gradient_hbm, gradient_in, head, 1).wait()
-        finish_forward(*members[0])
-        for head, slot in members:
-            backward_scores(head, slot)
-            if slot + 1 < together:
-                finish_forward(*members[slot + 1])
-            backward_products(head, slot)
+            repeat(head)
+
+        wide_copy(gradient_hbm, gradient_in, head, 1).wait()
+
+    def work_alone(head, carry):
+        forward_scores(head)
+        arrive(head, 1)
+        forward_products(head)
+        check(head)
+
+        @pl.when(head + 1 < heads)
+        def _():
+            arrive_queries(head + 1)
+
+        finish_forward(head)
+        backward_scores(head)
+        prepare(jnp.minimum(head + 1, heads - 1), (head + 1) % 3)
+        backward_products(head)
         return carry
 
-    if heads == together:
-        work(0, 0)
+    if heads < 3:
+        arrive_queries(0)
+        prepare(0, 0)
+        for head in range(1, heads):
+            start_copies(head)
+        lax.fori_loop(0, heads, work_alone, 0)
     else:
-        lax.fori_loop(0, heads // together, work, 0)
+        for head in range(1, heads):
+            start_copies(head)
+        for head in range(2):
+            arrive_queries(head)
+            prepare(head, head)
+        arrive(0, 1)
+        forward_scores(0)
+        forward_products(0)
+
+        def work(head, carry):
+            check(head)
+            arrive(head + 1, 1)
+
+            @pl.when(head + 2 < heads)
+            def _():
+                arrive_queries(head + 2)
+
+            finish_forward(head)
+            forward_scores(head + 1)
+            backward_scores(head)
+            prepare(jnp.minimum(head + 2, heads - 1), (head + 2) % 3)
+            forward_products(head + 1)
+            backward_products(head)
+            return carry
+
+        lax.fori_loop(0, heads - 1, work, 0)
+        check(heads - 1)
+        finish_forward(heads - 1)
+        backward_scores(heads - 1)
+        backward_products(heads - 1)
     up_copies = []
     for head in range(heads):
         at = pl.ds((start + head) * GROUP_WIDTH, GROUP_WIDTH)
@@ -469,7 +503,7 @@
 
 
 def attention_chunk(
-    first, last, together, columns, query_base, gradient, received, shared, tables, carried
+    first, last, columns, query_base, gradient, received, shared, tables, carried
 ):
     count = last - first
     tokens = query_base.shape[0]
@@ -505,11 +539,11 @@
             pltpu.VMEM((3, RANK, tokens), jnp.bfloat16),
             pltpu.VMEM((count, keys, wide_buf), jnp.bfloat16),
             pltpu.VMEM((count, keys, wide_buf), jnp.bfloat16),
-            pltpu.VMEM((together, rows, wide_buf), jnp.bfloat16),
-            pltpu.VMEM((together, rows, wide_buf), jnp.bfloat16),
-            pltpu.VMEM((together, rows, keys), jnp.bfloat16),
-            pltpu.VMEM((together, rows, keys), jnp.bfloat16),
-            pltpu.VMEM((together, rows, wide_buf), jnp.float32),
+            pltpu.VMEM((3, rows, wide_buf), jnp.bfloat16),
+            pltpu.VMEM((1, rows, wide_buf), jnp.bfloat16),
+            pltpu.VMEM((2, rows, keys), jnp.bfloat16),
+            pltpu.VMEM((1, rows, keys), jnp.bfloat16),
+            pltpu.VMEM((2, rows, wide_buf), jnp.float32),
             pltpu.SemaphoreType.DMA((10,)),
             pltpu.SemaphoreType.DMA((count, 4, 4)),
         ],
@@ -672,7 +706,6 @@
         *carried, = attention_chunk(
             first,
             last,
-            TOGETHER[chunk],
             columns,
             query_base,
             output_gradient,

time: 201 us -> 198 us (0.985)
  Pallas kernels: 123 us -> 120 us
    pallas_call x3, Pallas kernels: 118 us -> 115 us  [attention_chunk(): pl.pallas_call(functools.partial(attention_kernel, carried is None, first...]
where the time goes in v3:
time: 198 us; the launch traced here: 197 us
  Pallas kernels  120 us (61%)
  starting transfers between devices  47.6 us (24%)
  waiting for transfers between devices  24.6 us (12%)
  matrix products  2.9 us (1%)
    pallas_call x3, Pallas kernels, attention_chunk(): pl.pallas_call(functools.partial(attention_kernel, carried is None, first...  115 us
    ppermute x8, waiting for transfers between devices, exchange(): lax.ppermute(value, 'ctx', [(i, i ^ distance) for i in range(devices)])  13 us
    ppermute x3, starting transfers between devices, per_device(): odd = lax.ppermute(one, 'ctx', even_one)  12 us
    ppermute x3, starting transfers between devices, per_device(): evens.append(lax.ppermute(own, 'ctx', even_two))  11.1 us
    ppermute x8, starting transfers between devices, exchange(): lax.ppermute(value, 'ctx', [(i, i ^ distance) for i in range(devices)])  10.5 us
    ppermute x3, starting transfers between devices, per_device(): ones.append(lax.ppermute(own, 'ctx', forward_one))  6.81 us
    ppermute x2, starting transfers between devices, head_sum(): other = lax.ppermute(x, 'head', [(0, 1), (1, 0)])  4.55 us
    ppermute x2, waiting for transfers between devices, head_sum(): other = lax.ppermute(x, 'head', [(0, 1), (1, 0)])  3.98 us
  transfers between devices with their start and end apart: 21, of which 11 were waited for; matrix products, arithmetic and copies ran while one was open for 0% of the time, Pallas kernels for 38%

profile of v3, /device:TPU:0, one launch (start us, length us, event | category | flops | bytes accessed | tf_op | source)
XLA Modules:
  0.0 197.1 jit_solution(17731361762697004684)
XLA Ops:
  0.7 2.9 %fusion = f32[32,512]{1,0:T(8,128)S(1)} fusion(bf16[512,2688]{1,0:T(8,128)(2,1)} %hidden_ref.1, bf16[2688,16]{0,1:T(8,128)(2,1)} %param.18, bf16[2688,16]{0,1:T(8,128)(2,1)} %param.16), kind=kOutput, calls=%fused_computation.1 | convolution fusion | flops 88424448 | bytes 2990080 | tf_op jit(solution)/shard_map/dot_general | solution.py:39
  3.6 3.0 %collective-permute-start = (f32[32,512]{1,0:T(8,128)S(1)}, f32[32,512]{1,0:T(8,128)S(1)}, u32[]{:S(2)}, u32[]{:S(2)}) collective-permute-start(f32[32,512]{1,0:T(8,128)S(1)} %fusion), channel_id=1, source_target_pairs={{0,1},{1,0},{2,3},{3,2},{4,5},{5,4},{6,7},{7,6},{8,9},{9,8},{10,11... | collective-permute-start | bytes 196616 | tf_op jit(solution)/shard_map/ppermute | solution.py:596
  7.7 1.1 collective-permute-done
  8.8 4.0 %collective-permute-start.2 = (bf16[528,512]{1,0:T(8,128)(2,1)S(1)}, bf16[528,512]{1,0:T(8,128)(2,1)S(1)}, u32[]{:S(2)}, u32[]{:S(2)}) collective-permute-start(bf16[528,512]{1,0:T(8,128)(2,1)S(1)} %get-tuple-element.58.refs_2_), channel_id=1, source_target_pairs={{0,4},{4,8},{8,12},{12,16},{16,20},{20,24},{24,28},{1,5},{5,9},{9,... | collective-permute-start | bytes 1622024 | tf_op jit(solution)/shard_map/ppermute | solution.py:693
  12.8 1.3 collective-permute-start.6
  14.2 1.8 shard_map.156
  16.0 4.1 %collective-permute-start.1 = (bf16[512,768]{1,0:T(8,128)(2,1)S(1)}, bf16[512,768]{1,0:T(8,128)(2,1)S(1)}, u32[]{:S(2)}, u32[]{:S(2)}) collective-permute-start(bf16[512,768]{1,0:T(8,128)(2,1)S(1)} %get-tuple-element.35.refs_2_), channel_id=1, source_target_pairs={{0,2},{2,4},{4,6},{6,8},{8,10},{10,12},{12,14},{14,16},{16,18},{18... | collective-permute-start | bytes 2359304 | tf_op jit(solution)/shard_map/ppermute | solution.py:692
  20.1 3.4 %collective-permute-start.5 = (bf16[512,768]{1,0:T(8,128)(2,1)S(1)}, bf16[512,768]{1,0:T(8,128)(2,1)S(1)}, u32[]{:S(2)}, u32[]{:S(2)}) collective-permute-start(bf16[512,768]{1,0:T(8,128)(2,1)S(1)} %get-tuple-element.35.refs_2_), channel_id=1, source_target_pairs={{0,4},{4,8},{8,12},{12,16},{16,20},{20,24},{24,28},{1,5},{5,9},{9,... | collective-permute-start | bytes 2359304 | tf_op jit(solution)/shard_map/ppermute | solution.py:693
  23.6 4.7 %collective-permute-start.7 = (bf16[528,512]{1,0:T(8,128)(2,1)S(1)}, bf16[528,512]{1,0:T(8,128)(2,1)S(1)}, u32[]{:S(2)}, u32[]{:S(2)}) collective-permute-start(bf16[528,512]{1,0:T(8,128)(2,1)S(1)} %collective-permute-done.6.refs_3_), channel_id=1, source_target_pairs={{0,2},{4,6},{8,10},{12,14},{16,18},{20,22},{24,26},{28,30},{1,3},{... | collective-permute-start | bytes 1622024 | tf_op jit(solution)/shard_map/ppermute | solution.py:705
  28.3 1.5 collective-permute-done.7.refs_5_
  29.8 29.6 %shard_map.157 = (bf16[512,2048]{1,0:T(8,128)(2,1)}, bf16[16,8704]{1,0:T(8,128)(2,1)S(1)}, f32[64,512]{1,0:T(8,128)S(1)}, bf16[1536,128]{1,0:T(8,128)(2,1)S(1)}) custom-call(bf16[512,2048]{1,0:T(8,128)(2,1)S(1)} %copy-done.1, bf16[512,2048]{1,0:T(8,128)(2,1)S(1)} %copy-done.2, bf16[528,512]{1,0:T(8,128)(2,1)S(1)} %get-tuple-element.58.refs_2_, ...), custom_call_target="tpu_custom_call" | custom-call | tf_op jit(solution)/shard_map/pallas_call | solution.py:529
  59.4 2.4 %collective-permute-start.8 = (bf16[512,768]{1,0:T(8,128)(2,1)S(1)}, bf16[512,768]{1,0:T(8,128)(2,1)S(1)}, u32[]{:S(2)}, u32[]{:S(2)}) collective-permute-start(bf16[512,768]{1,0:T(8,128)(2,1)S(1)} %collective-permute-done.1.refs_3_), channel_id=1, source_target_pairs={{0,2},{4,6},{8,10},{12,14},{16,18},{20,22},{24,26},{28,30},{1,3},{... | collective-permute-start | bytes 2359304 | tf_op jit(solution)/shard_map/ppermute | solution.py:705
  61.8 3.7 %collective-permute-start.4 = (bf16[512,768]{1,0:T(8,128)(2,1)S(1)}, bf16[512,768]{1,0:T(8,128)(2,1)S(1)}, u32[]{:S(2)}, u32[]{:S(2)}) collective-permute-start(bf16[512,768]{1,0:T(8,128)(2,1)S(1)} %get-tuple-element.36.refs_2_), channel_id=1, source_target_pairs={{0,4},{4,8},{8,12},{12,16},{16,20},{20,24},{24,28},{1,5},{5,9},{9,... | collective-permute-start | bytes 2359304 | tf_op jit(solution)/shard_map/ppermute | solution.py:693
  65.5 1.3 collective-permute-start.3
  66.8 42.6 %shard_map.158 = (bf16[512,2048]{1,0:T(8,128)(2,1)}, bf16[16,8704]{1,0:T(8,128)(2,1)S(1)}, f32[64,512]{1,0:T(8,128)S(1)}) custom-call(bf16[512,2048]{1,0:T(8,128)(2,1)S(1)} %copy-done.1, bf16[512,2048]{1,0:T(8,128)(2,1)S(1)} %copy-done.2, bf16[512,768]{1,0:T(8,128)(2,1)S(1)} %get-tuple-element.35.refs_2_, ...), custom_call_target="tpu_custom_call", output_to_operand_aliasing={{0}: (13, {}), {1}: (14, {})} | custom-call | tf_op jit(solution)/shard_map/pallas_call | solution.py:529
  109.4 5.0 %collective-permute-start.9 = (bf16[512,768]{1,0:T(8,128)(2,1)S(1)}, bf16[512,768]{1,0:T(8,128)(2,1)S(1)}, u32[]{:S(2)}, u32[]{:S(2)}) collective-permute-start(bf16[512,768]{1,0:T(8,128)(2,1)S(1)} %collective-permute-done.3.refs_3_), channel_id=1, source_target_pairs={{0,2},{4,6},{8,10},{12,14},{16,18},{20,22},{24,26},{28,30},{1,3},{... | collective-permute-start | bytes 2359304 | tf_op jit(solution)/shard_map/ppermute | solution.py:705
  114.4 1.8 collective-permute-done.9.refs_5_
  116.3 42.6 %shard_map.159 = (bf16[512,2048]{1,0:T(8,128)(2,1)}, bf16[16,8704]{1,0:T(8,128)(2,1)S(1)}, f32[64,512]{1,0:T(8,128)S(1)}) custom-call(bf16[512,2048]{1,0:T(8,128)(2,1)S(1)} %copy-done.1, bf16[512,2048]{1,0:T(8,128)(2,1)S(1)} %copy-done.2, bf16[512,768]{1,0:T(8,128)(2,1)S(1)} %get-tuple-element.36.refs_2_, ...), custom_call_target="tpu_custom_call", output_to_operand_aliasing={{0}: (13, {}), {1}: (14, {})} | custom-call | tf_op jit(solution)/shard_map/pallas_call | solution.py:529
  158.9 1.6 collective-permute-start.10
  160.5 2.9 %collective-permute-done.10 = bf16[64,512]{1,0:T(8,128)(2,1)S(1)} collective-permute-done((bf16[64,512]{1,0:T(8,128)(2,1)S(1)}, bf16[64,512]{1,0:T(8,128)(2,1)S(1)}, u32[]{:S(2)}, u32[]{:S(2)}) %collective-permute-start.10) | collective-permute-done | bytes 65568 | tf_op jit(solution)/shard_map/ppermute | solution.py:596
  163.3 1.3 collective-permute-start.11
  164.6 1.3 collective-permute-start.12
  166.4 3.9 %collective-permute-done.12.two_ref = bf16[16,512]{1,0:T(8,128)(2,1)S(1)} collective-permute-done((bf16[16,512]{1,0:T(8,128)(2,1)S(1)}, bf16[16,512]{1,0:T(8,128)(2,1)S(1)}, u32[]{:S(2)}, u32[]{:S(2)}) %collective-permute-start.12) | collective-permute-done | bytes 16416 | tf_op jit(solution)/shard_map/ppermute | solution.py:725
  171.2 1.2 collective-permute-done.13
  172.5 2.8 %collective-permute-start.14 = (bf16[16,2176]{1,0:T(8,128)(2,1)S(1)}, bf16[16,2176]{1,0:T(8,128)(2,1)S(1)}, u32[]{:S(2)}, u32[]{:S(2)}) collective-permute-start(bf16[16,2176]{1,0:T(8,128)(2,1)S(1)} %constant_dynamic-slice_fusion), channel_id=1, source_target_pairs={{0,4},{2,6},{4,0},{6,2},{8,12},{10,14},{12,8},{14,10},{16,20},{18,... | collective-permute-start | bytes 208904 | tf_op jit(solution)/shard_map/ppermute | solution.py:606
  175.3 2.5 %collective-permute-done.14 = bf16[16,2176]{1,0:T(8,128)(2,1)S(1)} collective-permute-done((bf16[16,2176]{1,0:T(8,128)(2,1)S(1)}, bf16[16,2176]{1,0:T(8,128)(2,1)S(1)}, u32[]{:S(2)}, u32[]{:S(2)}) %collective-permute-start.14) | collective-permute-done | bytes 69664 | tf_op jit(solution)/shard_map/ppermute | solution.py:606
  177.8 2.4 %collective-permute-start.15 = (bf16[16,2176]{1,0:T(8,128)(2,1)S(1)}, bf16[16,2176]{1,0:T(8,128)(2,1)S(1)}, u32[]{:S(2)}, u32[]{:S(2)}) collective-permute-start(bf16[16,2176]{1,0:T(8,128)(2,1)S(1)} %add_convert_fusion.2), channel_id=1, source_target_pairs={{0,8},{2,10},{4,12},{6,14},{8,0},{10,2},{12,4},{14,6},{16,24},{18,... | collective-permute-start | bytes 208904 | tf_op jit(solution)/shard_map/ppermute | solution.py:606
  180.2 2.2 %collective-permute-start.16 = (bf16[16,2176]{1,0:T(8,128)(2,1)S(1)}, bf16[16,2176]{1,0:T(8,128)(2,1)S(1)}, u32[]{:S(2)}, u32[]{:S(2)}) collective-permute-start(bf16[16,2176]{1,0:T(8,128)(2,1)S(1)} %add_convert_fusion.2), channel_id=1, source_target_pairs={{0,16},{2,18},{4,20},{6,22},{8,24},{10,26},{12,28},{14,30},{16,0},... | collective-permute-start | bytes 208904 | tf_op jit(solution)/shard_map/ppermute | solution.py:606
  183.4 5.4 %collective-permute-done.16 = bf16[16,2176]{1,0:T(8,128)(2,1)S(1)} collective-permute-done((bf16[16,2176]{1,0:T(8,128)(2,1)S(1)}, bf16[16,2176]{1,0:T(8,128)(2,1)S(1)}, u32[]{:S(2)}, u32[]{:S(2)}) %collective-permute-start.16) | collective-permute-done | bytes 69664 | tf_op jit(solution)/shard_map/ppermute | solution.py:606
  188.9 1.3 collective-permute-start.19
  190.8 3.1 %collective-permute-done.19.refs_2_ = bf16[16,2176]{1,0:T(8,128)(2,1)S(1)} collective-permute-done((bf16[16,2176]{1,0:T(8,128)(2,1)S(1)}, bf16[16,2176]{1,0:T(8,128)(2,1)S(1)}, u32[]{:S(2)}, u32[]{:S(2)}) %collective-permute-start.19) | collective-permute-done | bytes 69664 | tf_op jit(solution)/shard_map/ppermute | solution.py:606
  195.3 1.8 shard_map.161
  (58 shorter events, 5.8 us)
Async XLA Ops:
  0.6 27.7 %copy-start = (bf16[16,1024]{1,0:T(8,128)(2,1)S(1)}, bf16[16,1024]{1,0:T(8,128)(2,1)}, u32[]{:S(2)}) copy-start(bf16[16,1024]{1,0:T(8,128)(2,1)} %param.19) | copy-start | bytes 98308
  0.6 5.9 %copy-start.6 = (f32[64,1]{1,0:T(8,128)S(1)}, f32[64,1]{1,0:T(8,128)}, u32[]{:S(2)}) copy-start(f32[64,1]{1,0:T(8,128)} %constant.52.clone.frequency_ref) | copy-start | bytes 772
  0.7 5.9 %copy-start.8 = (s32[512]{0:T(512)S(1)}, s32[512]{0:T(512)}, u32[]{:S(2)}) copy-start(s32[512]{0:T(512)} %param.20) | copy-start | bytes 6148
  0.7 5.9 %copy-start.4 = (bf16[512,1024]{1,0:T(8,128)(2,1)S(1)}, bf16[512,1024]{1,0:T(8,128)(2,1)}, u32[]{:S(2)}) copy-start(bf16[512,1024]{1,0:T(8,128)(2,1)} %key_ref.3) | copy-start | bytes 3145732
  0.7 5.9 %copy-start.5 = (bf16[512,1024]{1,0:T(8,128)(2,1)S(1)}, bf16[512,1024]{1,0:T(8,128)(2,1)}, u32[]{:S(2)}) copy-start(bf16[512,1024]{1,0:T(8,128)(2,1)} %value_ref.3) | copy-start | bytes 3145732
  0.7 13.5 %copy-start.7 = (s32[64,9]{0,1:T(8,128)S(1)}, s32[64,9]{0,1:T(8,128)}, u32[]{:S(2)}) copy-start(s32[64,9]{0,1:T(8,128)} %param.21) | copy-start | bytes 6916
  3.6 5.2 %collective-permute-start = (f32[32,512]{1,0:T(8,128)S(1)}, f32[32,512]{1,0:T(8,128)S(1)}, u32[]{:S(2)}, u32[]{:S(2)}) collective-permute-start(f32[32,512]{1,0:T(8,128)S(1)} %fusion), channel_id=1, source_target_pairs={{0,1},{1,0},{2,3},{3,2},{4,5},{5,4},{6,7},{7,6},{8,9},{9,8},{10,11... | collective-permute-start | bytes 196616 | tf_op jit(solution)/shard_map/ppermute | solution.py:596
  6.6 21.7 %copy-start.13 = (bf16[16,2048]{1,0:T(8,128)(2,1)S(1)}, bf16[16,2048]{1,0:T(8,128)(2,1)}, u32[]{:S(2)}) copy-start(bf16[16,2048]{1,0:T(8,128)(2,1)} %param.17) | copy-start | bytes 196612
  6.6 23.2 %copy-start.1 = (bf16[512,2048]{1,0:T(8,128)(2,1)S(1)}, bf16[512,2048]{1,0:T(8,128)(2,1)}, u32[]{:S(2)}) copy-start(bf16[512,2048]{1,0:T(8,128)(2,1)} %refs_0_.5) | copy-start | bytes 6291460
  6.6 23.2 %copy-start.2 = (bf16[512,2048]{1,0:T(8,128)(2,1)S(1)}, bf16[512,2048]{1,0:T(8,128)(2,1)}, u32[]{:S(2)}) copy-start(bf16[512,2048]{1,0:T(8,128)(2,1)} %refs_1_.5) | copy-start | bytes 6291460
  8.8 14.7 %collective-permute-start.2 = (bf16[528,512]{1,0:T(8,128)(2,1)S(1)}, bf16[528,512]{1,0:T(8,128)(2,1)S(1)}, u32[]{:S(2)}, u32[]{:S(2)}) collective-permute-start(bf16[528,512]{1,0:T(8,128)(2,1)S(1)} %get-tuple-element.58.refs_2_), channel_id=1, source_target_pairs={{0,4},{4,8},{8,12},{12,16},{16,20},{20,24},{24,28},{1,5},{5,9},{9,... | collective-permute-start | bytes 1622024 | tf_op jit(solution)/shard_map/ppermute | solution.py:693
  12.8 10.8 %collective-permute-start.6 = (bf16[528,512]{1,0:T(8,128)(2,1)S(1)}, bf16[528,512]{1,0:T(8,128)(2,1)S(1)}, u32[]{:S(2)}, u32[]{:S(2)}) collective-permute-start(bf16[528,512]{1,0:T(8,128)(2,1)S(1)} %get-tuple-element.58.refs_2_), channel_id=1, source_target_pairs={{0,2},{2,4},{4,6},{6,8},{8,10},{10,12},{12,14},{14,16},{16,18},{18... | collective-permute-start | bytes 1622024 | tf_op jit(solution)/shard_map/ppermute | solution.py:692
  16.0 43.4 %collective-permute-start.1 = (bf16[512,768]{1,0:T(8,128)(2,1)S(1)}, bf16[512,768]{1,0:T(8,128)(2,1)S(1)}, u32[]{:S(2)}, u32[]{:S(2)}) collective-permute-start(bf16[512,768]{1,0:T(8,128)(2,1)S(1)} %get-tuple-element.35.refs_2_), channel_id=1, source_target_pairs={{0,2},{2,4},{4,6},{6,8},{8,10},{10,12},{12,14},{14,16},{16,18},{18... | collective-permute-start | bytes 2359304 | tf_op jit(solution)/shard_map/ppermute | solution.py:692
  20.1 39.3 %collective-permute-start.5 = (bf16[512,768]{1,0:T(8,128)(2,1)S(1)}, bf16[512,768]{1,0:T(8,128)(2,1)S(1)}, u32[]{:S(2)}, u32[]{:S(2)}) collective-permute-start(bf16[512,768]{1,0:T(8,128)(2,1)S(1)} %get-tuple-element.35.refs_2_), channel_id=1, source_target_pairs={{0,4},{4,8},{8,12},{12,16},{16,20},{20,24},{24,28},{1,5},{5,9},{9,... | collective-permute-start | bytes 2359304 | tf_op jit(solution)/shard_map/ppermute | solution.py:693
  23.6 6.2 %collective-permute-start.7 = (bf16[528,512]{1,0:T(8,128)(2,1)S(1)}, bf16[528,512]{1,0:T(8,128)(2,1)S(1)}, u32[]{:S(2)}, u32[]{:S(2)}) collective-permute-start(bf16[528,512]{1,0:T(8,128)(2,1)S(1)} %collective-permute-done.6.refs_3_), channel_id=1, source_target_pairs={{0,2},{4,6},{8,10},{12,14},{16,18},{20,22},{24,26},{28,30},{1,3},{... | collective-permute-start | bytes 1622024 | tf_op jit(solution)/shard_map/ppermute | solution.py:705
  59.4 7.4 %collective-permute-start.8 = (bf16[512,768]{1,0:T(8,128)(2,1)S(1)}, bf16[512,768]{1,0:T(8,128)(2,1)S(1)}, u32[]{:S(2)}, u32[]{:S(2)}) collective-permute-start(bf16[512,768]{1,0:T(8,128)(2,1)S(1)} %collective-permute-done.1.refs_3_), channel_id=1, source_target_pairs={{0,2},{4,6},{8,10},{12,14},{16,18},{20,22},{24,26},{28,30},{1,3},{... | collective-permute-start | bytes 2359304 | tf_op jit(solution)/shard_map/ppermute | solution.py:705
  61.8 47.6 %collective-permute-start.4 = (bf16[512,768]{1,0:T(8,128)(2,1)S(1)}, bf16[512,768]{1,0:T(8,128)(2,1)S(1)}, u32[]{:S(2)}, u32[]{:S(2)}) collective-permute-start(bf16[512,768]{1,0:T(8,128)(2,1)S(1)} %get-tuple-element.36.refs_2_), channel_id=1, source_target_pairs={{0,4},{4,8},{8,12},{12,16},{16,20},{20,24},{24,28},{1,5},{5,9},{9,... | collective-permute-start | bytes 2359304 | tf_op jit(solution)/shard_map/ppermute | solution.py:693
  65.5 44.0 %collective-permute-start.3 = (bf16[512,768]{1,0:T(8,128)(2,1)S(1)}, bf16[512,768]{1,0:T(8,128)(2,1)S(1)}, u32[]{:S(2)}, u32[]{:S(2)}) collective-permute-start(bf16[512,768]{1,0:T(8,128)(2,1)S(1)} %get-tuple-element.36.refs_2_), channel_id=1, source_target_pairs={{0,2},{2,4},{4,6},{6,8},{8,10},{10,12},{12,14},{14,16},{16,18},{18... | collective-permute-start | bytes 2359304 | tf_op jit(solution)/shard_map/ppermute | solution.py:692
  109.4 6.9 %collective-permute-start.9 = (bf16[512,768]{1,0:T(8,128)(2,1)S(1)}, bf16[512,768]{1,0:T(8,128)(2,1)S(1)}, u32[]{:S(2)}, u32[]{:S(2)}) collective-permute-start(bf16[512,768]{1,0:T(8,128)(2,1)S(1)} %collective-permute-done.3.refs_3_), channel_id=1, source_target_pairs={{0,2},{4,6},{8,10},{12,14},{16,18},{20,22},{24,26},{28,30},{1,3},{... | collective-permute-start | bytes 2359304 | tf_op jit(solution)/shard_map/ppermute | solution.py:705
  116.3 54.0 %copy-start.3 = (bf16[512,2688]{1,0:T(8,128)(2,1)S(1)}, bf16[512,2688]{1,0:T(8,128)(2,1)}, u32[]{:S(2)}) copy-start(bf16[512,2688]{1,0:T(8,128)(2,1)} %hidden_ref.1) | copy-start | bytes 8257540
  158.9 4.4 %collective-permute-start.10 = (bf16[64,512]{1,0:T(8,128)(2,1)S(1)}, bf16[64,512]{1,0:T(8,128)(2,1)S(1)}, u32[]{:S(2)}, u32[]{:S(2)}) collective-permute-start(bf16[64,512]{1,0:T(8,128)(2,1)S(1)} %convert_element_type.49), channel_id=1, source_target_pairs={{0,1},{1,0},{2,3},{3,2},{4,5},{5,4},{6,7},{7,6},{8,9},{9,8},{10,11... | collective-permute-start | bytes 196616 | tf_op jit(solution)/shard_map/ppermute | solution.py:596
  163.3 3.1 %collective-permute-start.11 = (bf16[16,512]{1,0:T(8,128)(2,1)S(1)}, bf16[16,512]{1,0:T(8,128)(2,1)S(1)}, u32[]{:S(2)}, u32[]{:S(2)}) collective-permute-start(bf16[16,512]{1,0:T(8,128)(2,1)S(1)} %get-tuple-element.56), channel_id=1, source_target_pairs={{2,0},{4,2},{6,4},{8,6},{10,8},{12,10},{14,12},{16,14},{18,16},{20... | collective-permute-start | bytes 49160 | tf_op jit(solution)/shard_map/ppermute | solution.py:722
  164.6 5.6 %collective-permute-start.12 = (bf16[16,512]{1,0:T(8,128)(2,1)S(1)}, bf16[16,512]{1,0:T(8,128)(2,1)S(1)}, u32[]{:S(2)}, u32[]{:S(2)}) collective-permute-start(bf16[16,512]{1,0:T(8,128)(2,1)S(1)} %get-tuple-element.55), channel_id=1, source_target_pairs={{4,0},{6,2},{8,4},{10,6},{12,8},{14,10},{16,12},{18,14},{20,16},{2... | collective-permute-start | bytes 49160 | tf_op jit(solution)/shard_map/ppermute | solution.py:725
  171.0 1.4 collective-permute-start.13
  172.5 5.2 %collective-permute-start.14 = (bf16[16,2176]{1,0:T(8,128)(2,1)S(1)}, bf16[16,2176]{1,0:T(8,128)(2,1)S(1)}, u32[]{:S(2)}, u32[]{:S(2)}) collective-permute-start(bf16[16,2176]{1,0:T(8,128)(2,1)S(1)} %constant_dynamic-slice_fusion), channel_id=1, source_target_pairs={{0,4},{2,6},{4,0},{6,2},{8,12},{10,14},{12,8},{14,10},{16,20},{18,... | collective-permute-start | bytes 208904 | tf_op jit(solution)/shard_map/ppermute | solution.py:606
  177.8 5.6 %collective-permute-start.15 = (bf16[16,2176]{1,0:T(8,128)(2,1)S(1)}, bf16[16,2176]{1,0:T(8,128)(2,1)S(1)}, u32[]{:S(2)}, u32[]{:S(2)}) collective-permute-start(bf16[16,2176]{1,0:T(8,128)(2,1)S(1)} %add_convert_fusion.2), channel_id=1, source_target_pairs={{0,8},{2,10},{4,12},{6,14},{8,0},{10,2},{12,4},{14,6},{16,24},{18,... | collective-permute-start | bytes 208904 | tf_op jit(solution)/shard_map/ppermute | solution.py:606
  180.2 8.6 %collective-permute-start.16 = (bf16[16,2176]{1,0:T(8,128)(2,1)S(1)}, bf16[16,2176]{1,0:T(8,128)(2,1)S(1)}, u32[]{:S(2)}, u32[]{:S(2)}) collective-permute-start(bf16[16,2176]{1,0:T(8,128)(2,1)S(1)} %add_convert_fusion.2), channel_id=1, source_target_pairs={{0,16},{2,18},{4,20},{6,22},{8,24},{10,26},{12,28},{14,30},{16,0},... | collective-permute-start | bytes 208904 | tf_op jit(solution)/shard_map/ppermute | solution.py:606
  182.3 6.5 %collective-permute-start.17 = (bf16[16,2176]{1,0:T(8,128)(2,1)S(1)}, bf16[16,2176]{1,0:T(8,128)(2,1)S(1)}, u32[]{:S(2)}, u32[]{:S(2)}) collective-permute-start(bf16[16,2176]{1,0:T(8,128)(2,1)S(1)} %add_convert_fusion.2), channel_id=1, source_target_pairs={{0,24},{2,26},{4,28},{6,30},{8,16},{10,18},{12,20},{14,22},{16,8},... | collective-permute-start | bytes 208904 | tf_op jit(solution)/shard_map/ppermute | solution.py:606
  188.9 5.8 %copy-start.9 = (bf16[16,2176]{1,0:T(8,128)(2,1)}, bf16[16,2176]{1,0:T(8,128)(2,1)S(1)}, u32[]{:S(2)}) copy-start(bf16[16,2176]{1,0:T(8,128)(2,1)S(1)} %add_convert_fusion.1.refs_0_) | copy-start | bytes 208900
  188.9 1.9 collective-permute-start.18
  188.9 5.0 %collective-permute-start.19 = (bf16[16,2176]{1,0:T(8,128)(2,1)S(1)}, bf16[16,2176]{1,0:T(8,128)(2,1)S(1)}, u32[]{:S(2)}, u32[]{:S(2)}) collective-permute-start(bf16[16,2176]{1,0:T(8,128)(2,1)S(1)} %add_convert_fusion.1.refs_0_), channel_id=1, source_target_pairs={{0,4},{2,6},{4,0},{6,2},{8,12},{10,14},{12,8},{14,10},{16,20},{18,... | collective-permute-start | bytes 208904 | tf_op jit(solution)/shard_map/ppermute | solution.py:606
  190.2 4.4 %collective-permute-start.20 = (bf16[16,2176]{1,0:T(8,128)(2,1)S(1)}, bf16[16,2176]{1,0:T(8,128)(2,1)S(1)}, u32[]{:S(2)}, u32[]{:S(2)}) collective-permute-start(bf16[16,2176]{1,0:T(8,128)(2,1)S(1)} %add_convert_fusion.1.refs_0_), channel_id=1, source_target_pairs={{0,6},{2,4},{4,2},{6,0},{8,14},{10,12},{12,10},{14,8},{16,22},{18,... | collective-permute-start | bytes 208904 | tf_op jit(solution)/shard_map/ppermute | solution.py:606
  (3 other events, 5.3 us)
